TPU v7x, 128 devices: a whole 4x4x4 slice. The times are simulated.
128 devices in a mesh: visit: 16 (over z, y_lo, core), grp: 8 (over x, y_hi).
Axes of the slice: x: 4, y: 4 (y_hi: 2, y_lo: 2; y = y_hi * 2 + y_lo), z: 4, core: 2. Of those that a mesh axis runs over, the one named last changes fastest.
Arguments:
- coadd_tiles: float32 [4096, 16384], P('visit', 'grp'), may hold values from -9 to 9
- science: float32 [4096, 16384], P('visit', 'grp'), may hold values from -16 to 16
- correlation: int32 [16], P('visit'), may hold values from 0 to 15, as said below
- offset: int32 [16], P('visit'), may hold values from 10 to 246
Outputs:
- difference: float32 [4096, 16384], P('visit', 'grp')
- significance: float32 [4096, 16384], P('visit', 'grp')
- match_coef: float32 [16, 6], P('visit')
Inputs may be any that keep to these rules, and one draw needn't show every extreme that they name: correlation is a permutation of 0 .. 15.
All inputs are finite; a program needn't handle non-finite values.
Results may differ from a plain program's by a relative error of at most 0.0003.
Values sent between devices are 32-bit elements; how exact they have to be, the bound alone decides.
No kernel may reach another device: no remote copies, remote signals or barrier semaphores. Data moves between devices by JAX's collectives and lax.ppermute only.
A program may use at most 128 MiB of HBM per device.

v0:
```python
import jax
import jax.numpy as jnp
from jax import lax
from jax.sharding import Mesh
from jax.sharding import PartitionSpec as P

ROWS = 256
COLS = 2048
KER_HALF = 10
BASIS = 5
FILT_HALF = 6
GRP = ("grp_0", "grp_1")


ridge = 0.05
epsilon = 1e-06


def sent_to_all(x, axis):
    size = lax.axis_size(axis)
    return lax.all_to_all(jnp.broadcast_to(x[None], (size, *x.shape)), axis, 0, 0, tiled=True)


def laid_out(blocks, dim):
    lengths = list(blocks.shape[1:])
    lengths[dim] *= blocks.shape[0]
    return jnp.moveaxis(blocks, 0, dim).reshape(lengths)


def gather_directly(x, axis, dim):
    blocks = sent_to_all(x, axis)
    return laid_out(blocks, dim)


def extended(x, sides, width):
    for axis, dim in sides:
        size, length = (lax.axis_size(axis), x.shape[dim])
        up = [(i, (i + 1) % size) for i in range(size - 1)]
        down = [(j, i) for i, j in up]
        last = lax.slice_in_dim(x, length - width, length, axis=dim)
        initial = lax.slice_in_dim(x, 0, width, axis=dim)
        before = lax.ppermute(last, axis, up)
        after = lax.ppermute(initial, axis, down)
        x = jnp.concatenate([before, x, after], axis=dim)
    return x


def by_axis(x, axes):
    for axis in axes:
        x = lax.psum(x, axis)
    return x


def gauss_taps(spread, half_width):
    points = jnp.arange(-half_width, half_width + 1).astype(jnp.float32)
    return jnp.exp(-points * points / (2.0 * spread * spread))


def basis_taps():
    points = jnp.arange(-KER_HALF, KER_HALF + 1).astype(jnp.float32)
    narrow = gauss_taps(1.0, KER_HALF)
    middle = gauss_taps(1.8, KER_HALF)
    wide_gauss = gauss_taps(3.2, KER_HALF)
    slope_taps = points * middle / 1.8
    row_taps = jnp.stack([narrow, middle, wide_gauss, slope_taps, middle])
    col_taps = jnp.stack([narrow, middle, wide_gauss, middle, slope_taps])
    scales = jnp.sqrt(jnp.sum(row_taps * row_taps, 1) * jnp.sum(col_taps * col_taps, 1))
    return (row_taps / scales[:, None], col_taps)


def filter_taps():
    smooth = gauss_taps(2.0, FILT_HALF)
    return smooth / jnp.sqrt(jnp.sum(smooth * smooth))


def taps_matrix(kernel_taps, step_len):
    half_width = (kernel_taps.shape[1] - 1) // 2
    input_pos = jnp.arange(step_len + 2 * half_width)[:, None]
    output_pos = jnp.arange(step_len)[None, :]
    distance = input_pos - output_pos
    inside = (distance >= 0) & (distance <= 2 * half_width)
    picked = kernel_taps[:, jnp.clip(distance, 0, 2 * half_width)]
    return jnp.where(inside[None], picked, 0.0)


def block_anchors(extent, step_len):
    anchors = list(range(0, extent - step_len + 1, step_len))
    leftover = extent - (anchors[-1] + step_len)
    return (anchors, leftover)


def joined(result, axis_pos):
    layout = result.shape
    merged = layout[:axis_pos] + (-1,) + layout[axis_pos + 2 :]
    return result.reshape(merged)


def along_cols(image_in, kernel_taps):
    half_width = (kernel_taps.shape[1] - 1) // 2
    extent = image_in.shape[1] - 2 * half_width
    step_len = min(256, extent)
    anchors, leftover = block_anchors(extent, step_len)
    windows = jnp.stack(
        [image_in[:, anchor : anchor + step_len + 2 * half_width] for anchor in anchors], 1
    )
    result = jnp.einsum(
        "hnk,ckm->chnm",
        windows,
        taps_matrix(kernel_taps, step_len),
        precision=lax.Precision.HIGHEST,
    )
    return joined(result, 2)


def along_rows(layers, kernel_taps):
    half_width = (kernel_taps.shape[1] - 1) // 2
    extent = layers.shape[1] - 2 * half_width
    step_len = min(256, extent)
    anchors, leftover = block_anchors(extent, step_len)
    windows = jnp.stack([layers for anchor in anchors], 1)
    result = jnp.einsum(
        "cnkw,ckm->cnmw",
        windows,
        taps_matrix(kernel_taps, step_len),
        precision=lax.Precision.HIGHEST,
    )
    return joined(result, 1)


def build_normal(gram_matrix, basis_sums, counted):
    upper_rows = jnp.concatenate([gram_matrix, basis_sums[:, None]], 1)
    lower_row = jnp.concatenate([basis_sums, jnp.array([counted], jnp.float32)])[None]
    return jnp.concatenate([upper_rows, lower_row], 0) / counted + ridge * jnp.eye(
        BASIS + 1, dtype=jnp.float32
    )


def shards(coadd_tiles, science, correlation, offset):
    row_taps, col_taps = basis_taps()
    smooth = filter_taps()[None]
    visits = lax.axis_size("visit")
    groups = lax.axis_size(GRP)
    shift_rows = offset[0]
    span_rows = ROWS + 2 * KER_HALF
    piece_rows = ROWS // visits
    held_pieces = lax.all_to_all(
        coadd_tiles.reshape(visits, piece_rows, COLS),
        "visit",
        split_axis=0,
        concat_axis=0,
        tiled=True,
    )
    all_ids = gather_directly(correlation, "visit", 0)
    holders = jnp.arange(visits)[None, :]
    first_pick = (all_ids[:, None] == holders).astype(jnp.float32)
    second_pick = (((all_ids + 1) % visits)[:, None] == holders).astype(jnp.float32)
    selector = jnp.stack([first_pick, second_pick], 0)
    outgoing = jnp.einsum("tvh,hrc->tvrc", selector, held_pieces, precision=lax.Precision.HIGHEST)
    arrived = lax.all_to_all(outgoing, "visit", split_axis=1, concat_axis=1, tiled=True)
    window = lax.dynamic_slice_in_dim(
        arrived.reshape(2 * ROWS, COLS), shift_rows - KER_HALF, span_rows, 0
    )
    margin = KER_HALF
    framed = extended(window, ((GRP, 1),), margin)
    matched = along_rows(along_cols(framed, col_taps), row_taps)
    basis_flat = matched.reshape(BASIS, -1)
    gram_matrix = jnp.dot(basis_flat, basis_flat.T, precision=lax.Precision.HIGHEST)
    basis_sums = jnp.sum(basis_flat, 1)
    projection = jnp.dot(basis_flat, science.reshape(-1), precision=lax.Precision.HIGHEST)
    science_total = jnp.sum(science)
    gram_matrix, basis_sums, projection, science_total = (
        by_axis(gram_matrix, GRP),
        by_axis(basis_sums, GRP),
        by_axis(projection, GRP),
        by_axis(science_total, GRP),
    )
    counted = float(ROWS * COLS * groups)
    normal = build_normal(gram_matrix, basis_sums, counted)
    rhs_vector = jnp.concatenate([projection, science_total[None]]) / counted
    factor = jnp.linalg.cholesky(normal)
    halfway = lax.linalg.triangular_solve(factor, rhs_vector[:, None], left_side=True, lower=True)
    coefficients = lax.linalg.triangular_solve(
        factor, halfway, left_side=True, lower=True, transpose_a=True
    )[:, 0]
    difference = (
        science - jnp.sum(coefficients[:BASIS, None, None] * matched, 0) - coefficients[BASIS]
    )
    spread_diff = extended(difference, ((GRP, 1),), FILT_HALF)
    row_framed = jnp.pad(spread_diff, ((FILT_HALF, FILT_HALF), (0, 0)))
    filtered = along_rows(along_cols(row_framed, smooth), smooth)[0]
    noise_power = jnp.mean(difference * difference)
    significance = filtered / jnp.sqrt(noise_power + epsilon)
    return (difference, significance, coefficients[None])


def solution(mesh):
    split = Mesh(mesh.devices.reshape(mesh.shape["visit"], 4, 2), ("visit", "grp_0", "grp_1"))
    in_specs = (P("visit", GRP), P("visit", GRP), P("visit"), P("visit"))
    out_specs = (P("visit", GRP), P("visit", GRP), P("visit", None))
    return jax.shard_map(
        shards, mesh=split, in_specs=in_specs, out_specs=out_specs, check_vma=False
    )
```

profile of v0, /device:TPU:0, one launch (start us, length us, event | category | flops | bytes accessed | tf_op | source)
XLA Modules:
  0.0 799.6 jit_solution(2664910883539953847)
XLA Ops:
  1.3 12.4 %all_to_all.16 = s32[16,1,1]{2,1,0:T(1,128)S(1)} all-to-all(s32[16,1,1]{2,1,0:T(1,128)S(1)} %broadcast_in_dim.40), channel_id=1, replica_groups=mesh['visit'=16,'grp_0'=4,'grp_1'=2] {'visit'}, dimensions={0} | all-to-all | bytes 128 | tf_op jit(solution)/shard_map/all_to_all | solution.py:21
  13.7 3.7 all-to-all-start.1
  17.9 27.4 %all-to-all-done.1 = f32[16,16,2048]{2,1,0:T(8,128)S(1)} async-done(((f32[16,16,2048]{2,1,0:T(8,128)}), f32[16,16,2048]{2,1,0:T(8,128)S(1)}, u32[]{:S(2)}, u32[]{:S(2)}) %all-to-all-start.1) | async-done | bytes 2097184 | tf_op jit(solution)/shard_map/all_to_all | solution.py:146
  45.2 2.9 fusion.5
  48.1 4.4 copy.75
  52.5 4.5 all-to-all-start.2
  58.0 232.4 %gather_fusion.1 = f32[70656,5]{1,0:T(8,128)} fusion(f32[5,21]{0,1:T(8,128)S(1)} %copy.72, s32[70656]{0:T(1024)S(1)} %broadcast_clamp_fusion), kind=kCustom, calls=%fused_computation.1 | custom fusion | bytes 3108864 | tf_op jit(solution)/shard_map/gather | solution.py:82
  290.4 20.3 %copy.73 = f32[276,256,5]{1,0,2:T(8,128)} copy(f32[276,256,5]{2,1,0:T(8,128)} %bitcast.248) | data formatting | bytes 2826240 | tf_op jit(solution)/shard_map/gather | solution.py:82
  311.1 232.4 %gather_fusion = f32[70656,5]{1,0:T(8,128)} fusion(f32[5,21]{0,1:T(8,128)S(1)} %copy.70, s32[70656]{0:T(1024)S(1)} %broadcast_clamp_fusion), kind=kCustom, calls=%fused_computation | custom fusion | bytes 3108864 | tf_op jit(solution)/shard_map/gather | solution.py:82
  543.5 20.4 %copy.71 = f32[276,256,5]{1,0,2:T(8,128)} copy(f32[276,256,5]{2,1,0:T(8,128)} %bitcast.247) | data formatting | bytes 2826240 | tf_op jit(solution)/shard_map/gather | solution.py:82
  567.2 2.5 copy.76
  569.8 4.8 collective-permute-start
  574.9 1.5 collective-permute-start.1
  576.4 1.6 collective-permute-done
  579.4 4.5 collective-permute-done.1
  584.2 21.1 %convolution_bitcast_fusion = f32[5,276,8,256]{3,1,2,0:T(8,128)S(1)} fusion(f32[276,8,276]{2,0,1:T(8,128)S(1)} %fusion.27, f32[276,256,5]{1,0,2:T(8,128)S(1)} %copy-done.5, pred[276,256]{1,0:T(8,128)(4,1)S(1)} %copy-done.6), kind=kOutput, calls=%fused_computation.7 | convolution fusion | flops 9360860160 | bytes 15226368 | tf_op jit(solution)/shard_map/hnk,ckm->chnm/dot_general | solution.py:106
  605.2 7.8 copy.77
  613.0 10.9 %reshape.361 = f32[5,276,2048]{2,1,0:T(8,128)} reshape(f32[5,276,8,256]{3,2,1,0:T(8,128)} %copy.77) | data formatting | bytes 22609920 | tf_op jit(solution)/shard_map/reshape.16
  623.9 20.5 %fusion.156 = (f32[5]{0:T(128)S(1)}, f32[5,256,2048]{2,1,0:T(8,128)S(1)}) fusion(f32[5,276,2048]{2,1,0:T(8,128)} %reshape.361, f32[276,256,5]{1,0,2:T(8,128)S(1)} %copy-done.4, pred[276,256]{1,0:T(8,128)(4,1)S(1)} %copy-done.7), kind=kOutput, calls=%fused_computation.206 | convolution fusion | flops 8685184000 | bytes 23274516 | tf_op jit(solution)/shard_map/cnkw,ckm->cnmw/dot_general | solution.py:121
  644.4 36.2 %fusion.14 = f32[5,5]{0,1:T(8,128)S(1)} fusion(f32[5,256,2048]{2,1,0:T(8,128)S(1)} %get-tuple-element.31), kind=kOutput, calls=%fused_computation.31 | convolution fusion | flops 157286400 | bytes 10485860 | tf_op jit(solution)/shard_map/dot_general | solution.py:167
  680.6 44.0 %fusion.17 = f32[5]{0:T(128)S(1)} fusion(f32[256,2048,1]{1,0,2:T(8,128)S(1)} %bitcast.257, f32[5,256,2048]{2,1,0:T(8,128)} %copy-done), kind=kOutput, calls=%fused_computation.32 | convolution fusion | flops 31457280 | bytes 12582932 | tf_op jit(solution)/shard_map/dot_general | solution.py:169
  724.6 11.2 %all-reduce.1 = (f32[5]{0:T(128)S(1)}, f32[5,5]{0,1:T(8,128)S(1)}, f32[]{:T(128)}, f32[5]{0:T(128)S(1)}) all-reduce(f32[5]{0:T(128)S(1)} %get-tuple-element.30, f32[5,5]{0,1:T(8,128)S(1)} %fusion.14, f32[]{:T(128)} %reduce_sum.66, f32[5]{0:T(128)S(1)} %fusion.17), channel_id=1, replica_groups=mesh['visit'=16,'grp_0'=4,'grp_1'=2] {'grp_0'}, use_global_device_ids=true, to_apply=%region_5.6 | all-reduce | flops 36 | bytes 288 | tf_op jit(solution)/shard_map/psum | solution.py:50
  735.8 7.1 all-reduce.2
  747.6 5.6 multiply_reduce_fusion
  753.2 1.9 multiply_reduce_fusion.1
  755.1 1.3 copy-done.3
  756.5 3.1 collective-permute-start.2
  759.6 1.3 collective-permute-start.3
  762.4 5.6 collective-permute-done.3
  768.0 3.2 concatenate.29
  771.5 12.2 %convolution_bitcast_fusion.1 = f32[1,268,8,256]{3,1,2,0:T(8,128)S(1)} fusion(f32[268,8,268]{2,0,1:T(8,128)S(1)} %fusion.51, f32[]{:T(128)} %bitcast.50, f32[]{:T(128)} %bitcast.51, f32[]{:T(128)} %bitcast.52, f32[]{:T(128)} %bitcast.53, f32[]{:T(128)} %bitcast.54, f32[]{:T(128)} %bitcast.56, f32[]{:T(128)} %bitcast.55, f32[]{:T(128)} %bitcast.39, ...), kind=kOutput, calls=%fused_computation.25 | convolution fusion | flops 1767479296 | bytes 4493876 | tf_op jit(solution)/shard_map/hnk,ckm->chnm/dot_general | solution.py:106
  786.2 13.0 %convolution_divide_fusion = f32[256,2048]{1,0:T(8,128)} fusion(f32[268,2048]{1,0:T(8,128)S(1)} %bitcast.260, f32[]{:T(128)S(6)} %sqrt.15, f32[]{:T(128)} %bitcast.50, f32[]{:T(128)} %bitcast.51, f32[]{:T(128)} %bitcast.52, f32[]{:T(128)} %bitcast.53, f32[]{:T(128)} %bitcast.54, f32[]{:T(128)} %bitcast.56, f32[]{:T(128)} %bitcast.55, f32[]{:T(128)} %bitcast.39, ...), kind=kOutput, calls=%fused_computation.9 | convolution fusion | flops 1688967168 | bytes 4292664 | tf_op jit(solution)/shard_map/cnkw,ckm->cnmw/dot_general | solution.py:121
  (78 shorter events, 13.7 us)
Async XLA Ops:
  13.7 31.6 %all-to-all-start.1 = ((f32[16,16,2048]{2,1,0:T(8,128)}), f32[16,16,2048]{2,1,0:T(8,128)S(1)}, u32[]{:S(2)}, u32[]{:S(2)}) async-start(f32[16,16,2048]{2,1,0:T(8,128)} %bitcast.261), calls=%async_computation.1 | async-start | bytes 4194304 | tf_op jit(solution)/shard_map/all_to_all | solution.py:146
  52.5 514.7 %all-to-all-start.2 = ((f32[2,16,16,2048]{3,2,0,1:T(8,128)}), f32[2,16,16,2048]{3,2,0,1:T(8,128)}, u32[]{:S(2)}, u32[]{:S(2)}) async-start(f32[2,16,16,2048]{3,2,0,1:T(8,128)} %copy.75), calls=%async_computation.2 | async-start | bytes 8388608 | tf_op jit(solution)/shard_map/all_to_all | solution.py:159
  543.5 21.9 %copy-start.1 = (f32[256,2048]{1,0:T(8,128)S(1)}, f32[256,2048]{1,0:T(8,128)}, u32[]{:S(2)}) copy-start(f32[256,2048]{1,0:T(8,128)} %param.6) | copy-start | bytes 6291460
  569.8 8.2 %collective-permute-start = (f32[276,10]{1,0:T(8,128)S(1)}, f32[276,10]{1,0:T(8,128)S(1)}, u32[]{:S(2)}, u32[]{:S(2)}) collective-permute-start(f32[276,10]{1,0:T(8,128)S(1)} %get-tuple-element.14), channel_id=1, source_target_pairs={{0,1},{1,2},{2,3},{3,4},{4,5},{5,6},{6,7},{8,9},{9,10},{10,11},{11... | collective-permute-start | bytes 33128 | tf_op jit(solution)/shard_map/ppermute | solution.py:42
  574.9 9.0 %collective-permute-start.1 = (f32[276,10]{1,0:T(8,128)S(1)}, f32[276,10]{1,0:T(8,128)S(1)}, u32[]{:S(2)}, u32[]{:S(2)}) collective-permute-start(f32[276,10]{1,0:T(8,128)S(1)} %get-tuple-element.13), channel_id=1, source_target_pairs={{1,0},{2,1},{3,2},{4,3},{5,4},{6,5},{7,6},{9,8},{10,9},{11,10},{12... | collective-permute-start | bytes 33128 | tf_op jit(solution)/shard_map/ppermute | solution.py:43
  578.6 5.6 copy-start.5
  578.6 5.6 copy-start.6
  613.0 10.9 %copy-start.4 = (f32[276,256,5]{1,0,2:T(8,128)S(1)}, f32[276,256,5]{1,0,2:T(8,128)}, u32[]{:S(2)}) copy-start(f32[276,256,5]{1,0,2:T(8,128)} %copy.71) | copy-start | bytes 4239364
  613.0 10.9 %copy-start.7 = (pred[276,256]{1,0:T(8,128)(4,1)S(1)}, pred[276,256]{1,0:T(8,128)(4,1)}, u32[]{:S(2)}) copy-start(pred[276,256]{1,0:T(8,128)(4,1)} %fusion.54) | copy-start | bytes 211972
  644.4 36.2 %copy-start = (f32[5,256,2048]{2,1,0:T(8,128)}, f32[5,256,2048]{2,1,0:T(8,128)S(1)}, u32[]{:S(2)}) copy-start(f32[5,256,2048]{2,1,0:T(8,128)S(1)} %get-tuple-element.31) | copy-start | bytes 31457284
  644.4 36.2 %copy-start.2 = (f32[256,2048]{1,0:T(8,128)S(1)}, f32[256,2048]{1,0:T(8,128)}, u32[]{:S(2)}) copy-start(f32[256,2048]{1,0:T(8,128)} %param.6) | copy-start | bytes 6291460
  747.0 6.2 copy-start.8
  755.1 1.3 copy-start.3
  756.5 5.9 collective-permute-start.2
  759.6 8.4 %collective-permute-start.3 = (f32[256,6]{1,0:T(8,128)S(1)}, f32[256,6]{1,0:T(8,128)S(1)}, u32[]{:S(2)}, u32[]{:S(2)}) collective-permute-start(f32[256,6]{1,0:T(8,128)S(1)} %get-tuple-element.15), channel_id=1, source_target_pairs={{1,0},{2,1},{3,2},{4,3},{5,4},{6,5},{7,6},{9,8},{10,9},{11,10},{12... | collective-permute-start | bytes 18440 | tf_op jit(solution)/shard_map/ppermute | solution.py:43
where the time goes:
time: 808 us; the launch traced here: 800 us
  local copies, waits for them, and re-layouts  542 us (67%)
  matrix products  151 us (19%)
  waiting for transfers between devices  39.1 us (5%)
  blocking collectives  30.7 us (4%)
  starting transfers between devices  19 us (2%)
  other arithmetic  14 us (2%)
    gather x5, local copies, waits for them, and re-layouts, taps_matrix(): picked = kernel_taps[:, jnp.clip(distance, 0, 2 * half_width)]  506 us
    dot_general x1, matrix products, shards(): jnp.dot(basis_flat, science.reshape(-1), precision=lax.Precision.HIGHEST)  44 us
    dot_general x1, matrix products, shards(): jnp.dot(basis_flat, basis_flat.T, precision=lax.Precision.HIGHEST)  36.2 us
    dot_general x2, matrix products, along_rows(): jnp.einsum('cnkw,ckm->cnmw', windows, taps_matrix(kernel_taps, step_len),...  33.5 us
    dot_general x2, matrix products, along_cols(): jnp.einsum('hnk,ckm->chnm', windows, taps_matrix(kernel_taps, step_len),...  33.3 us
    all_to_all x1, waiting for transfers between devices, shards(): lax.all_to_all(coadd_tiles.reshape(visits, piece_rows, COLS), 'visit', sp...  27.4 us
    psum x2, blocking collectives, by_axis(): x = lax.psum(x, axis)  18.3 us
  transfers between devices with their start and end apart: 6, of which 4 were waited for; matrix products, arithmetic and copies ran while one was open for 64% of the time, Pallas kernels for 0%

commit v1 on v0

v1 whole, which is shorter than its diff:
```python
import functools

import jax
import jax.numpy as jnp
import ml_dtypes
import numpy as np
from jax import lax
from jax.experimental import pallas as pl
from jax.experimental.pallas import tpu as pltpu
from jax.sharding import Mesh
from jax.sharding import PartitionSpec as P

ROWS = 256
COLS = 2048
KER_HALF = 10
BASIS = 5
FILT_HALF = 6
GRP = ("grp_0", "grp_1")
LANES = 128
HALF = 64
BLOCKS = COLS // LANES
TILES = BLOCKS + 1
WIN = 280
WIN_PAD = 288
SENT = ROWS + 8
STRIP = BLOCKS * ROWS
BAND = 160
FBAND = 144
NSUMS = 32

ridge = 0.05
epsilon = 1e-06
bf16 = jnp.bfloat16
f32 = jnp.float32
VMEM = pl.BlockSpec(memory_space=pltpu.VMEM)
SMEM = pl.BlockSpec(memory_space=pltpu.SMEM)


def params(mib):
    return pltpu.CompilerParams(vmem_limit_bytes=mib * 1024 * 1024)


def gauss_taps(spread, half_width):
    points = np.arange(-half_width, half_width + 1).astype(np.float64)
    return np.exp(-points * points / (2.0 * spread * spread))


def basis_taps():
    points = np.arange(-KER_HALF, KER_HALF + 1).astype(np.float64)
    narrow, middle, wide = (gauss_taps(s, KER_HALF) for s in (1.0, 1.8, 3.2))
    slope = points * middle / 1.8
    row = np.stack([narrow, middle, wide, slope, middle])
    col = np.stack([narrow, middle, wide, middle, slope])
    scales = np.sqrt((row * row).sum(1) * (col * col).sum(1))
    return row / scales[:, None], np.stack([narrow, middle, wide, slope])


def banded(taps, distance):
    half = (len(taps) - 1) // 2
    inside = np.abs(distance) <= half
    return np.where(inside, taps[np.clip(distance + half, 0, 2 * half)], 0.0)


def halves(matrix):
    matrix = matrix.astype(np.float32)
    high = matrix.astype(ml_dtypes.bfloat16)
    low = (matrix - high.astype(np.float32)).astype(ml_dtypes.bfloat16)
    return high, low


def constants():
    row, col = basis_taps()
    k, n = np.arange(2 * LANES)[:, None], np.arange(LANES)[None, :]
    shift = k - HALF - n
    high, low = halves(np.concatenate([banded(c, shift) for c in col], 1))
    col_mat = np.concatenate([high, high, low], 0)
    i, k = np.arange(LANES)[:, None], np.arange(BAND)[None, :]
    high, low = halves(np.concatenate([banded(row[b], k - i - KER_HALF) for b in (0, 1, 3, 2, 4)], 0))
    row_mat = np.concatenate([high, low, high], 1)
    smooth = gauss_taps(2.0, FILT_HALF)
    smooth = smooth / np.sqrt((smooth * smooth).sum())
    high, low = halves(banded(smooth, shift))
    fcol_mat = np.concatenate([high, high, low], 0)
    k = np.arange(FBAND)[None, :]
    high, low = halves(np.concatenate([banded(smooth, k - i), banded(smooth, k - 16 - i)], 0))
    frow_mat = np.concatenate([high, low, high], 1)
    return col_mat, row_mat, fcol_mat, frow_mat


COL_MAT, ROW_MAT, FCOL_MAT, FROW_MAT = constants()


def split(x):
    high = x.astype(bf16)
    return high, (x - high.astype(f32)).astype(bf16)


def pack_kernel(tile_id, shift, coadd, out):
    lane = lax.broadcasted_iota(jnp.int32, (8, LANES), 1)
    meta = jnp.where(lane == 0, tile_id[0].astype(f32), shift[0].astype(f32))
    for h in range(BLOCKS):
        out[h, :ROWS] = coadd[:, h * LANES : (h + 1) * LANES]
        out[h, ROWS:] = meta


def pick_kernel(meta, held, out, strip):
    for u in range(BLOCKS):
        strip[u * ROWS : (u + 1) * ROWS] = held[u, :ROWS]
    strip[STRIP : STRIP + ROWS] = held[0, :ROWS]
    strip[STRIP + ROWS :] = held[1, :8]

    def one(v, carry):
        first = meta[v, 0] * ROWS + meta[v, 1] - KER_HALF
        out[v] = strip[pl.ds(first, WIN), :]
        return carry

    lax.fori_loop(0, BLOCKS, one, 0)


def frame_kernel(science, left, right, out):
    def block(t):
        if t < 0:
            return left[...]
        if t == BLOCKS:
            return right[...]
        return science[:, t * LANES : (t + 1) * LANES]

    for t in range(TILES):
        out[t] = jnp.concatenate([block(t - 1)[:, HALF:], block(t)[:, :HALF]], 1)


def match_kernel(win, left, right, sci, col_mat, row_mat, matched, sums, xh, xl, acc):
    pad = jnp.zeros((WIN_PAD - WIN, LANES), f32)
    for t in range(TILES + 1):
        x = left[...] if t == 0 else right[...] if t == TILES else win[t - 1]
        xh[t], xl[t] = split(jnp.concatenate([x, pad], 0))
    acc[...] = jnp.zeros_like(acc)
    lane = lax.broadcasted_iota(jnp.int32, (8, LANES), 1)

    def layers(t):
        a_hi = jnp.concatenate([xh[t], xh[t + 1]], 1)
        a_lo = jnp.concatenate([xl[t], xl[t + 1]], 1)
        y = jnp.dot(jnp.concatenate([a_hi, a_lo, a_hi], 1), col_mat[...], preferred_element_type=f32)
        return split(y)

    def rows_of(ts):
        ys = [layers(t) for t in ts]
        for f, bases in enumerate(((0,), (1, 3), (2,), (4,))):
            lo = (0, 1, 3, 4)[f] * LANES
            lhs = row_mat[lo : lo + len(bases) * LANES, :]
            y_hi = jnp.concatenate([y[0][:, f * LANES : (f + 1) * LANES] for y in ys], 1)
            y_lo = jnp.concatenate([y[1][:, f * LANES : (f + 1) * LANES] for y in ys], 1)
            for r in range(2):
                part = slice(r * LANES, r * LANES + BAND)
                rhs = jnp.concatenate([y_hi[part], y_hi[part], y_lo[part]], 0)
                m = jnp.dot(lhs, rhs, preferred_element_type=f32)
                for i, b in enumerate(bases):
                    for s, t in enumerate(ts):
                        matched[b, t, r * LANES : (r + 1) * LANES] = m[i * LANES : (i + 1) * LANES, s * LANES : (s + 1) * LANES]

    def gram(t, keep):
        parts = [acc[k] for k in range(26)]
        for i in range(ROWS // 8):
            rows = slice(i * 8, i * 8 + 8)
            m = [matched[b, t, rows] for b in range(BASIS)]
            d = sci[t, rows]
            if keep is not None:
                m = [jnp.where(keep, x, 0.0) for x in m]
                d = jnp.where(keep, d, 0.0)
            k = 0
            for b in range(BASIS):
                for c in range(b, BASIS):
                    parts[k] = parts[k] + m[b] * m[c]
                    k += 1
            for b in range(BASIS):
                parts[15 + b] = parts[15 + b] + m[b]
                parts[20 + b] = parts[20 + b] + m[b] * d
            parts[25] = parts[25] + d
        for k in range(26):
            acc[k] = parts[k]

    def pair(p, carry):
        rows_of((2 * p, 2 * p + 1))

        @pl.when(p > 0)
        def _():
            gram(2 * p, None)

        @pl.when(p == 0)
        def _():
            gram(0, lane >= HALF)

        gram(2 * p + 1, None)
        return carry

    lax.fori_loop(0, TILES // 2, pair, 0)
    rows_of((TILES - 1,))
    gram(TILES - 1, lane < HALF)
    rows = [jnp.sum(acc[k], axis=0, keepdims=True) for k in range(26)]
    rows = jnp.concatenate(rows + [jnp.zeros((NSUMS - 26, LANES), f32)], 0)
    sums[...] = jnp.broadcast_to(jnp.sum(rows, axis=1, keepdims=True), (NSUMS, LANES))


def solve(total, counted):
    def entry(k):
        return total[k : k + 1] / counted

    m, k = {}, 0
    for b in range(BASIS):
        for c in range(b, BASIS):
            m[b, c] = entry(k)
            k += 1
    for b in range(BASIS):
        m[b, BASIS] = entry(15 + b)
    m[BASIS, BASIS] = jnp.ones((1, LANES), f32)
    n = BASIS + 1
    for b in range(n):
        m[b, b] = m[b, b] + ridge
    rhs = [entry(20 + b) for b in range(BASIS)] + [entry(25)]
    inv = []
    for a in range(n):
        inv.append(1.0 / m[a, a])
        for b in range(a + 1, n):
            factor = m[a, b] * inv[a]
            for c in range(b, n):
                m[b, c] = m[b, c] - factor * m[a, c]
            rhs[b] = rhs[b] - factor * rhs[a]
    out = [None] * n
    for a in reversed(range(n)):
        value = rhs[a]
        for b in range(a + 1, n):
            value = value - m[a, b] * out[b]
        out[a] = value * inv[a]
    return out


def finish_kernel(counted, groups, mine, other, matched, sci, fcol_mat, frow_mat, diff, sig, coef, dh, dl, eh, el, keep):
    c = solve(mine[...] + other[...], counted)
    lane = lax.broadcasted_iota(jnp.int32, (1, LANES), 1)
    coef_row = c[0]
    for b in range(1, BASIS + 1):
        coef_row = jnp.where(lane == b, c[b], coef_row)
    coef[...] = coef_row[:, : BASIS + 1]
    g = lax.axis_index(GRP[0]) * lax.axis_size(GRP[1]) + lax.axis_index(GRP[1])
    low_ok = jnp.where(g > 0, 1.0, 0.0).astype(f32)
    high_ok = jnp.where(g < groups - 1, 1.0, 0.0).astype(f32)
    low_mask = jnp.where(lane >= HALF, 1.0, low_ok)
    high_mask = jnp.where(lane < HALF, 1.0, high_ok)

    def one(t, power):
        d = sci[t] - c[BASIS]
        total = c[0] * matched[0, t]
        for b in range(1, BASIS):
            total = total + c[b] * matched[b, t]
        d = d - total
        d = d * jnp.where(t == 0, low_mask, jnp.where(t == TILES - 1, high_mask, 1.0))
        keep[t] = d
        dh[t], dl[t] = split(d)
        own = jnp.where((t == 0) & (lane < HALF), 0.0, jnp.where((t == TILES - 1) & (lane >= HALF), 0.0, 1.0))
        return power + jnp.sum((d * d * own).reshape(ROWS // 8, 8, LANES), axis=0)

    power = lax.fori_loop(0, TILES, one, jnp.zeros((8, LANES), f32))
    noise = jnp.sum(jnp.sum(power, axis=0, keepdims=True), axis=1, keepdims=True) / float(ROWS * COLS)
    scale = 1.0 / jnp.sqrt(jnp.broadcast_to(noise, (1, LANES)) + epsilon)

    def along_rows(ts):
        d_hi = jnp.concatenate([dh[t] for t in ts], 1)
        d_lo = jnp.concatenate([dl[t] for t in ts], 1)
        for r in range(2):
            part = slice(0, FBAND) if r == 0 else slice(ROWS - FBAND, ROWS)
            rhs = jnp.concatenate([d_hi[part], d_hi[part], d_lo[part]], 0)
            e = jnp.dot(frow_mat[r * LANES : (r + 1) * LANES, :], rhs, preferred_element_type=f32)
            e_hi, e_lo = split(e)
            for s, t in enumerate(ts):
                eh[t, r * LANES : (r + 1) * LANES] = e_hi[:, s * LANES : (s + 1) * LANES]
                el[t, r * LANES : (r + 1) * LANES] = e_lo[:, s * LANES : (s + 1) * LANES]

    def rows_pair(p, carry):
        along_rows((2 * p, 2 * p + 1))
        return carry

    lax.fori_loop(0, TILES // 2, rows_pair, 0)
    along_rows((TILES - 1,))
    for j in range(BLOCKS):
        e_hi = jnp.concatenate([eh[j], eh[j + 1]], 1)
        e_lo = jnp.concatenate([el[j], el[j + 1]], 1)
        s = jnp.dot(jnp.concatenate([e_hi, e_lo, e_hi], 1), fcol_mat[...], preferred_element_type=f32)
        sig[:, j * LANES : (j + 1) * LANES] = s * scale
        diff[:, j * LANES : (j + 1) * LANES] = jnp.concatenate([keep[j][:, HALF:], keep[j + 1][:, :HALF]], 1)


def call(kernel, ins, outs, scratch=(), mib=48, flops=0, nbytes=0):
    return pl.pallas_call(
        kernel,
        out_shape=outs,
        in_specs=ins,
        out_specs=jax.tree.map(lambda _: VMEM, outs),
        scratch_shapes=list(scratch),
        compiler_params=params(mib),
        cost_estimate=pl.CostEstimate(flops=flops, bytes_accessed=nbytes, transcendentals=0),
    )


def shape(*dims, dtype=f32):
    return jax.ShapeDtypeStruct(dims, dtype)


def line(size):
    up = [(i, i + 1) for i in range(size - 1)]
    return up, [(j, i) for i, j in up]


def shards(coadd, science, correlation, offset):
    groups = lax.axis_size(GRP)
    up, down = line(groups)
    sent = call(pack_kernel, [SMEM, SMEM, VMEM], shape(BLOCKS, SENT, LANES), nbytes=4 << 20)(correlation, offset, coadd)
    held = lax.all_to_all(sent, "visit", 0, 0, tiled=True)
    sci_left = lax.ppermute(science[:, COLS - LANES :], GRP, up)
    sci_right = lax.ppermute(science[:, :LANES], GRP, down)
    framed = call(frame_kernel, [VMEM] * 3, shape(TILES, ROWS, LANES), nbytes=4 << 20)(science, sci_left, sci_right)
    meta = held[:, ROWS, :2].astype(jnp.int32)
    picked = call(
        pick_kernel, [SMEM, VMEM], shape(BLOCKS, WIN, LANES), [pltpu.VMEM((STRIP + ROWS + 8, LANES), f32)], nbytes=5 << 20
    )(meta, held)
    win = lax.all_to_all(picked, "visit", 0, 0, tiled=True)
    left = lax.ppermute(win[BLOCKS - 1], GRP, up)
    right = lax.ppermute(win[0], GRP, down)
    tile16 = pltpu.VMEM((TILES + 1, WIN_PAD, LANES), bf16)
    matched, sums = call(
        match_kernel,
        [VMEM] * 6,
        (shape(BASIS, TILES, ROWS, LANES), shape(NSUMS, LANES)),
        [tile16, tile16, pltpu.VMEM((26, 8, LANES), f32)],
        flops=8 << 30,
    )(win, left, right, framed, jnp.asarray(COL_MAT), jnp.asarray(ROW_MAT))
    for axis, swap in ((GRP[1], [(0, 1), (1, 0)]), (GRP[0], [(0, 1), (1, 0), (2, 3), (3, 2)])):
        sums = sums + lax.ppermute(sums, axis, swap)
    other = lax.ppermute(sums, GRP[0], [(0, 3), (3, 0), (1, 2), (2, 1)])
    block16 = pltpu.VMEM((TILES, ROWS, LANES), bf16)
    return call(
        functools.partial(finish_kernel, float(ROWS * COLS * groups), groups),
        [VMEM] * 6,
        (shape(ROWS, COLS), shape(ROWS, COLS), shape(1, BASIS + 1)),
        [block16] * 4 + [pltpu.VMEM((TILES, ROWS, LANES), f32)],
        flops=3 << 30,
    )(sums, other, matched, framed, jnp.asarray(FCOL_MAT), jnp.asarray(FROW_MAT))


def solution(mesh):
    split_mesh = Mesh(mesh.devices.reshape(mesh.shape["visit"], 4, 2), ("visit", "grp_0", "grp_1"))
    in_specs = (P("visit", GRP), P("visit", GRP), P("visit"), P("visit"))
    out_specs = (P("visit", GRP), P("visit", GRP), P("visit", None))
    return jax.shard_map(shards, mesh=split_mesh, in_specs=in_specs, out_specs=out_specs, check_vma=False)
```

time: 808 us -> 143 us (0.18)
  local copies, waits for them, and re-layouts: 542 us -> 1.66 us
  matrix products: 151 us -> 0 us
  blocking collectives: 30.7 us -> 67.3 us
  Pallas kernels: 0 us -> 34.6 us
  waiting for transfers between devices: 39.1 us -> 8.79 us
  other arithmetic: 14 us -> 0.02 us
  starting transfers between devices: 19 us -> 27.4 us
    gather x5 -> x0, local copies, waits for them, and re-layouts: 506 us -> none  [taps_matrix(): picked = kernel_taps[:, jnp.clip(distance, 0, 2 * half_width)]]
    dot_general x7 -> x0, matrix products: 150 us -> none  [the longest x1 44 us: shards(): jnp.dot(basis_flat, science.reshape(-1), precision=lax.Precision.HIGHEST)]
    all_to_all x1 -> x2, blocking collectives: 12.4 us -> 67.3 us  [the longest x1 34.8 us: shards(): held = lax.all_to_all(sent, 'visit', 0, 0, tiled=True)]
    pallas_call x0 -> x5, Pallas kernels: none -> 34.6 us  [the longest x1 20.7 us: shards(): call(match_kernel, [VMEM] * 6, (shape(BASIS, TILES, ROWS, LANES), shape(N...]
    all_to_all x2 -> x0, waiting for transfers between devices: 27.4 us -> none  [the longest x1 27.4 us: shards(): lax.all_to_all(coadd_tiles.reshape(visits, piece_rows, COLS), 'visit', sp...]
    psum x2 -> x0, blocking collectives: 18.3 us -> none  [by_axis(): x = lax.psum(x, axis)]
    ppermute x4 -> x7, starting transfers between devices: 10.7 us -> 27.4 us  [the longest x2 8.68 us: shards(): sums = sums + lax.ppermute(sums, axis, swap)]
    another operation x7 -> x0, local copies, waits for them, and re-layouts: 11.3 us -> none
  transfers between devices with their start and end apart: 6 -> 7, of which waited for: 4 -> 5; matrix products, arithmetic and copies ran while one was open for 64% -> 0% of each run, Pallas kernels for 0% -> 1%
where the time goes in v1:
time: 143 us; the launch traced here: 142 us
  blocking collectives  67.3 us (47%)
  Pallas kernels  34.6 us (24%)
  starting transfers between devices  27.4 us (19%)
  waiting for transfers between devices  8.79 us (6%)
  between operations  2.1 us (1%)
  local copies, waits for them, and re-layouts  1.66 us (1%)
    all_to_all x1, blocking collectives, shards(): held = lax.all_to_all(sent, 'visit', 0, 0, tiled=True)  34.8 us
    all_to_all x1, blocking collectives, shards(): win = lax.all_to_all(picked, 'visit', 0, 0, tiled=True)  32.6 us
    pallas_call x1, Pallas kernels, shards(): call(match_kernel, [VMEM] * 6, (shape(BASIS, TILES, ROWS, LANES), shape(N...  20.7 us
    pallas_call x1, Pallas kernels, shards(): call(functools.partial(finish_kernel, float(ROWS * COLS * groups), groups...  11.5 us
    ppermute x2, starting transfers between devices, shards(): sums = sums + lax.ppermute(sums, axis, swap)  8.68 us
    ppermute x1, starting transfers between devices, shards(): sci_left = lax.ppermute(science[:, COLS - LANES:], GRP, up)  6.47 us
    ppermute x1, starting transfers between devices, shards(): left = lax.ppermute(win[BLOCKS - 1], GRP, up)  6.06 us
    ppermute x1, starting transfers between devices, shards(): other = lax.ppermute(sums, GRP[0], [(0, 3), (3, 0), (1, 2), (2, 1)])  3.59 us
  transfers between devices with their start and end apart: 7, of which 5 were waited for; matrix products, arithmetic and copies ran while one was open for 0% of the time, Pallas kernels for 1%

profile of v1, /device:TPU:0, one launch (start us, length us, event | category | flops | bytes accessed | tf_op | source)
XLA Modules:
  0.0 141.9 jit_solution(7062322180722222652)
XLA Ops:
  1.9 0.0 copy-start.1
  1.9 1.6 %copy-done.1 = f32[256,2048]{1,0:T(8,128)S(1)} copy-done((f32[256,2048]{1,0:T(8,128)S(1)}, f32[256,2048]{1,0:T(8,128)}, u32[]{:S(2)}) %copy-start.1) | copy-done | bytes 2097176
  3.5 0.2 shard_map.103
  3.7 34.8 %all_to_all.10.held = f32[16,264,128]{2,1,0:T(8,128)S(1)} all-to-all(f32[16,264,128]{2,1,0:T(8,128)S(1)} %shard_map.103), channel_id=1, replica_groups=mesh['visit'=16,'grp_0'=4,'grp_1'=2] {'visit'}, dimensions={0} | all-to-all | bytes 4325376 | tf_op jit(solution)/shard_map/all_to_all | solution.py:317
  38.5 1.1 shard_map.104
  39.5 0.0 copy-start
  39.5 32.6 %all_to_all.11.win = f32[16,280,128]{2,1,0:T(8,128)S(1)} all-to-all(f32[16,280,128]{2,1,0:T(8,128)S(1)} %shard_map.104), channel_id=1, replica_groups=mesh['visit'=16,'grp_0'=4,'grp_1'=2] {'visit'}, dimensions={0} | all-to-all | bytes 4587520 | tf_op jit(solution)/shard_map/all_to_all | solution.py:325
  72.1 1.3 collective-permute-start.1
  73.4 6.1 %collective-permute-start = (f32[280,128]{1,0:T(8,128)S(1)}, f32[280,128]{1,0:T(8,128)S(1)}, u32[]{:S(2)}, u32[]{:S(2)}) collective-permute-start(f32[280,128]{1,0:T(8,128)S(1)} %get-tuple-element.8), channel_id=1, source_target_pairs={{0,1},{1,2},{2,3},{3,4},{4,5},{5,6},{6,7},{8,9},{9,10},{10,11},{11... | collective-permute-start | bytes 430088 | tf_op jit(solution)/shard_map/ppermute | solution.py:326
  79.5 0.0 copy-done
  79.5 1.3 collective-permute-start.3
  80.8 0.0 copy-start.4
  80.8 0.0 copy-start.5
  80.9 6.5 %collective-permute-start.2 = (f32[256,128]{1,0:T(8,128)S(1)}, f32[256,128]{1,0:T(8,128)S(1)}, u32[]{:S(2)}, u32[]{:S(2)}) collective-permute-start(f32[256,128]{1,0:T(8,128)S(1)} %get-tuple-element.10), channel_id=1, source_target_pairs={{0,1},{1,2},{2,3},{3,4},{4,5},{5,6},{6,7},{8,9},{9,10},{10,11},{11... | collective-permute-start | bytes 393224 | tf_op jit(solution)/shard_map/ppermute | solution.py:318
  87.3 0.8 collective-permute-done.3.right
  88.2 2.8 %collective-permute-done.2.left = f32[256,128]{1,0:T(8,128)S(1)} collective-permute-done((f32[256,128]{1,0:T(8,128)S(1)}, f32[256,128]{1,0:T(8,128)S(1)}, u32[]{:S(2)}, u32[]{:S(2)}) %collective-permute-start.2) | collective-permute-done | bytes 131104 | tf_op jit(solution)/shard_map/ppermute | solution.py:318
  91.0 1.2 shard_map.105.sci
  92.2 0.0 copy-done.6
  92.2 0.0 copy-start.2
  92.2 0.0 copy-start.3
  92.2 0.0 collective-permute-done.1.right
  92.2 0.0 collective-permute-done.left
  92.2 0.0 copy-done.4
  92.3 0.0 copy-done.5
  92.3 20.7 %shard_map.106 = (f32[5,17,256,128]{3,2,1,0:T(8,128)}, f32[32,128]{1,0:T(8,128)S(1)}) custom-call(f32[16,280,128]{2,1,0:T(8,128)} %copy-done.6, f32[280,128]{1,0:T(8,128)S(1)} %collective-permute-done.left, f32[280,128]{1,0:T(8,128)S(1)} %collective-permute-done.1.right, f32[17,256,128]{2,1,0:T(8,128)S(1)} %shard_map.105.sci, ...), custom_call_target="tpu_custom_call" | custom-call | flops 8589934592 | tf_op jit(solution)/shard_map/pallas_call | solution.py:329
  113.0 4.0 %collective-permute-start.4 = (f32[32,128]{1,0:T(8,128)S(1)}, f32[32,128]{1,0:T(8,128)S(1)}, u32[]{:S(2)}, u32[]{:S(2)}) collective-permute-start(f32[32,128]{1,0:T(8,128)S(1)} %get-tuple-element.5), channel_id=1, source_target_pairs={{0,1},{1,0},{2,3},{3,2},{4,5},{5,4},{6,7},{7,6},{8,9},{9,8},{10,11... | collective-permute-start | bytes 49160 | tf_op jit(solution)/shard_map/ppermute | solution.py:337
  117.0 1.7 %collective-permute-done.4 = f32[32,128]{1,0:T(8,128)S(1)} collective-permute-done((f32[32,128]{1,0:T(8,128)S(1)}, f32[32,128]{1,0:T(8,128)S(1)}, u32[]{:S(2)}, u32[]{:S(2)}) %collective-permute-start.4) | collective-permute-done | bytes 16416 | tf_op jit(solution)/shard_map/ppermute | solution.py:337
  118.7 4.7 %collective-permute-start.5 = (f32[32,128]{1,0:T(8,128)S(1)}, f32[32,128]{1,0:T(8,128)S(1)}, u32[]{:S(2)}, u32[]{:S(2)}) collective-permute-start(f32[32,128]{1,0:T(8,128)S(1)} %add.6), channel_id=1, source_target_pairs={{0,2},{2,0},{4,6},{6,4},{1,3},{3,1},{5,7},{7,5},{8,10},{10,8},{12,... | collective-permute-start | bytes 49160 | tf_op jit(solution)/shard_map/ppermute | solution.py:337
  123.4 1.7 %collective-permute-done.5 = f32[32,128]{1,0:T(8,128)S(1)} collective-permute-done((f32[32,128]{1,0:T(8,128)S(1)}, f32[32,128]{1,0:T(8,128)S(1)}, u32[]{:S(2)}, u32[]{:S(2)}) %collective-permute-start.5) | collective-permute-done | bytes 16416 | tf_op jit(solution)/shard_map/ppermute | solution.py:337
  125.1 3.6 %collective-permute-start.6 = (f32[32,128]{1,0:T(8,128)S(1)}, f32[32,128]{1,0:T(8,128)S(1)}, u32[]{:S(2)}, u32[]{:S(2)}) collective-permute-start(f32[32,128]{1,0:T(8,128)S(1)} %add.7.mine), channel_id=1, source_target_pairs={{0,6},{6,0},{2,4},{4,2},{1,7},{7,1},{3,5},{5,3},{8,14},{14,8},{10,... | collective-permute-start | bytes 49160 | tf_op jit(solution)/shard_map/ppermute | solution.py:338
  128.7 1.7 %collective-permute-done.6.other = f32[32,128]{1,0:T(8,128)S(1)} collective-permute-done((f32[32,128]{1,0:T(8,128)S(1)}, f32[32,128]{1,0:T(8,128)S(1)}, u32[]{:S(2)}, u32[]{:S(2)}) %collective-permute-start.6) | collective-permute-done | bytes 16416 | tf_op jit(solution)/shard_map/ppermute | solution.py:338
  130.4 11.5 %shard_map.107 = (f32[256,2048]{1,0:T(8,128)}, f32[256,2048]{1,0:T(8,128)}, f32[1,6]{1,0:T(1,128)}) custom-call(f32[32,128]{1,0:T(8,128)S(1)} %add.7.mine, f32[32,128]{1,0:T(8,128)S(1)} %collective-permute-done.6.other, f32[5,17,256,128]{3,2,1,0:T(8,128)} %get-tuple-element.6.matched, f32[17,256,128]{2,1,0:T(8,128)S(1)} %shard_map.105.sci, ...), custom_call_target="tpu_custom_call" | custom-call | flops 3221225472 | tf_op jit(solution)/shard_map/pallas_call | solution.py:340
  (8 shorter events, 0.1 us)
Async XLA Ops:
  1.9 1.6 %copy-start.1 = (f32[256,2048]{1,0:T(8,128)S(1)}, f32[256,2048]{1,0:T(8,128)}, u32[]{:S(2)}) copy-start(f32[256,2048]{1,0:T(8,128)} %coadd.1) | copy-start | bytes 6291460
  39.5 40.0 %copy-start = (f32[256,2048]{1,0:T(8,128)S(1)}, f32[256,2048]{1,0:T(8,128)}, u32[]{:S(2)}) copy-start(f32[256,2048]{1,0:T(8,128)} %science.1) | copy-start | bytes 6291460
  72.1 20.1 %copy-start.6 = (f32[16,280,128]{2,1,0:T(8,128)}, f32[16,280,128]{2,1,0:T(8,128)S(1)}, u32[]{:S(2)}) copy-start(f32[16,280,128]{2,1,0:T(8,128)S(1)} %all_to_all.11.win) | copy-start | bytes 6881284
  72.1 20.1 %collective-permute-start.1 = (f32[280,128]{1,0:T(8,128)S(1)}, f32[280,128]{1,0:T(8,128)S(1)}, u32[]{:S(2)}, u32[]{:S(2)}) collective-permute-start(f32[280,128]{1,0:T(8,128)S(1)} %get-tuple-element.7), channel_id=1, source_target_pairs={{1,0},{2,1},{3,2},{4,3},{5,4},{6,5},{7,6},{9,8},{10,9},{11,10},{12... | collective-permute-start | bytes 430088 | tf_op jit(solution)/shard_map/ppermute | solution.py:327
  73.4 18.8 %collective-permute-start = (f32[280,128]{1,0:T(8,128)S(1)}, f32[280,128]{1,0:T(8,128)S(1)}, u32[]{:S(2)}, u32[]{:S(2)}) collective-permute-start(f32[280,128]{1,0:T(8,128)S(1)} %get-tuple-element.8), channel_id=1, source_target_pairs={{0,1},{1,2},{2,3},{3,4},{4,5},{5,6},{6,7},{8,9},{9,10},{10,11},{11... | collective-permute-start | bytes 430088 | tf_op jit(solution)/shard_map/ppermute | solution.py:326
  79.5 8.6 %collective-permute-start.3 = (f32[256,128]{1,0:T(8,128)S(1)}, f32[256,128]{1,0:T(8,128)S(1)}, u32[]{:S(2)}, u32[]{:S(2)}) collective-permute-start(f32[256,128]{1,0:T(8,128)S(1)} %get-tuple-element.9), channel_id=1, source_target_pairs={{1,0},{2,1},{3,2},{4,3},{5,4},{6,5},{7,6},{9,8},{10,9},{11,10},{12... | collective-permute-start | bytes 393224 | tf_op jit(solution)/shard_map/ppermute | solution.py:319
  80.8 11.4 %copy-start.4 = (bf16[768,512]{1,0:T(8,128)(2,1)S(1)}, bf16[768,512]{1,0:T(8,128)(2,1)}, u32[]{:S(2)}) copy-start(bf16[768,512]{1,0:T(8,128)(2,1)} %constant.8.clone.col_mat) | copy-start | bytes 2359300
  80.8 11.4 %copy-start.5 = (bf16[640,480]{1,0:T(8,128)(2,1)S(1)}, bf16[640,480]{1,0:T(8,128)(2,1)}, u32[]{:S(2)}) copy-start(bf16[640,480]{1,0:T(8,128)(2,1)} %constant.9.clone.row_mat) | copy-start | bytes 1843204
  80.9 10.1 %collective-permute-start.2 = (f32[256,128]{1,0:T(8,128)S(1)}, f32[256,128]{1,0:T(8,128)S(1)}, u32[]{:S(2)}, u32[]{:S(2)}) collective-permute-start(f32[256,128]{1,0:T(8,128)S(1)} %get-tuple-element.10), channel_id=1, source_target_pairs={{0,1},{1,2},{2,3},{3,4},{4,5},{5,6},{6,7},{8,9},{9,10},{10,11},{11... | collective-permute-start | bytes 393224 | tf_op jit(solution)/shard_map/ppermute | solution.py:318
  92.2 38.2 %copy-start.2 = (bf16[256,432]{1,0:T(8,128)(2,1)S(1)}, bf16[256,432]{1,0:T(8,128)(2,1)}, u32[]{:S(2)}) copy-start(bf16[256,432]{1,0:T(8,128)(2,1)} %constant.11.clone.frow_mat) | copy-start | bytes 663556
  92.2 38.2 %copy-start.3 = (bf16[768,128]{1,0:T(8,128)(2,1)S(1)}, bf16[768,128]{1,0:T(8,128)(2,1)}, u32[]{:S(2)}) copy-start(bf16[768,128]{1,0:T(8,128)(2,1)} %constant.10.clone.fcol_mat) | copy-start | bytes 589828
  113.0 5.7 %collective-permute-start.4 = (f32[32,128]{1,0:T(8,128)S(1)}, f32[32,128]{1,0:T(8,128)S(1)}, u32[]{:S(2)}, u32[]{:S(2)}) collective-permute-start(f32[32,128]{1,0:T(8,128)S(1)} %get-tuple-element.5), channel_id=1, source_target_pairs={{0,1},{1,0},{2,3},{3,2},{4,5},{5,4},{6,7},{7,6},{8,9},{9,8},{10,11... | collective-permute-start | bytes 49160 | tf_op jit(solution)/shard_map/ppermute | solution.py:337
  118.7 6.4 %collective-permute-start.5 = (f32[32,128]{1,0:T(8,128)S(1)}, f32[32,128]{1,0:T(8,128)S(1)}, u32[]{:S(2)}, u32[]{:S(2)}) collective-permute-start(f32[32,128]{1,0:T(8,128)S(1)} %add.6), channel_id=1, source_target_pairs={{0,2},{2,0},{4,6},{6,4},{1,3},{3,1},{5,7},{7,5},{8,10},{10,8},{12,... | collective-permute-start | bytes 49160 | tf_op jit(solution)/shard_map/ppermute | solution.py:337
  125.1 5.3 %collective-permute-start.6 = (f32[32,128]{1,0:T(8,128)S(1)}, f32[32,128]{1,0:T(8,128)S(1)}, u32[]{:S(2)}, u32[]{:S(2)}) collective-permute-start(f32[32,128]{1,0:T(8,128)S(1)} %add.7.mine), channel_id=1, source_target_pairs={{0,6},{6,0},{2,4},{4,2},{1,7},{7,1},{3,5},{5,3},{8,14},{14,8},{10,... | collective-permute-start | bytes 49160 | tf_op jit(solution)/shard_map/ppermute | solution.py:338

commit v2 on v1

--- a/solution.py
+++ b/solution.py
@@ -27,6 +27,9 @@
 BAND = 160
 FBAND = 144
 NSUMS = 32
+EDGE = 16
+PAIRS = (TILES - 3) // 2
+PARTS = 4
 
 ridge = 0.05
 epsilon = 1e-06
@@ -95,44 +98,78 @@
     return high, (x - high.astype(f32)).astype(bf16)
 
 
-def pack_kernel(tile_id, shift, coadd, out):
-    lane = lax.broadcasted_iota(jnp.int32, (8, LANES), 1)
+def edge_kernel(coadd_first, coadd_last, sci_first, sci_last, to_left, to_right):
+    to_left[:EDGE] = jnp.transpose(coadd_first[...])[:EDGE]
+    to_left[EDGE:] = jnp.transpose(sci_first[...])[:EDGE]
+    to_right[:EDGE] = jnp.transpose(coadd_last[...])[LANES - EDGE :]
+    to_right[EDGE:] = jnp.transpose(sci_last[...])[LANES - EDGE :]
+
+
+def pack_kernel(tile_id, shift, coadd, from_left, from_right, out):
+    lane = lax.broadcasted_iota(jnp.int32, (4, LANES), 1)
     meta = jnp.where(lane == 0, tile_id[0].astype(f32), shift[0].astype(f32))
     for h in range(BLOCKS):
         out[h, :ROWS] = coadd[:, h * LANES : (h + 1) * LANES]
-        out[h, ROWS:] = meta
-
-
-def pick_kernel(meta, held, out, strip):
+        source = from_left if h < BLOCKS // 2 else from_right
+        k = 2 * h % EDGE
+        pieces = [source[k + i : k + i + 1, q * LANES : (q + 1) * LANES] for i in range(2) for q in range(2)]
+        out[h, ROWS:] = jnp.concatenate(pieces + [meta], 0)
+
+
+def pick_kernel(meta, held, out, strip, edges):
+    def keep_edges(u, at):
+        for i in range(2):
+            for q in range(2):
+                row = ROWS + 2 * i + q
+                edges[i : i + 1, at * ROWS + q * LANES : at * ROWS + (q + 1) * LANES] = held[u, row : row + 1]
+
+    edges[...] = jnp.zeros_like(edges)
     for u in range(BLOCKS):
         strip[u * ROWS : (u + 1) * ROWS] = held[u, :ROWS]
+        keep_edges(u, u)
     strip[STRIP : STRIP + ROWS] = held[0, :ROWS]
     strip[STRIP + ROWS :] = held[1, :8]
+    keep_edges(0, BLOCKS)
+    keep_edges(1, BLOCKS + 1)
 
     def one(v, carry):
-        first = meta[v, 0] * ROWS + meta[v, 1] - KER_HALF
-        out[v] = strip[pl.ds(first, WIN), :]
+        base = pl.multiple_of(meta[v, 0] * ROWS, ROWS)
+        skip = meta[v, 1] - KER_HALF
+        out[v, :WIN] = strip[pl.ds(base + skip, WIN), :]
+        wide = edges[:, pl.ds(base, 5 * LANES)]
+        wide = pltpu.roll(wide, 5 * LANES - skip, 1)
+        pieces = [wide[i : i + 1, q * LANES : (q + 1) * LANES] for i in range(2) for q in range(3)]
+        out[v, WIN:] = jnp.concatenate(pieces + [wide[2:4, :LANES]], 0)
         return carry
 
     lax.fori_loop(0, BLOCKS, one, 0)
 
 
-def frame_kernel(science, left, right, out):
+def frame_kernel(science, from_left, from_right, out, side):
+    side[...] = jnp.zeros_like(side)
+    side[:EDGE] = from_right[EDGE:]
+    side[LANES - EDGE :] = from_left[EDGE:]
+    edge = jnp.transpose(side[...])
+
     def block(t):
-        if t < 0:
-            return left[...]
-        if t == BLOCKS:
-            return right[...]
-        return science[:, t * LANES : (t + 1) * LANES]
+        return edge if t in (-1, BLOCKS) else science[:, t * LANES : (t + 1) * LANES]
 
     for t in range(TILES):
         out[t] = jnp.concatenate([block(t - 1)[:, HALF:], block(t)[:, :HALF]], 1)
 
 
-def match_kernel(win, left, right, sci, col_mat, row_mat, matched, sums, xh, xl, acc):
+def match_kernel(win, sci, col_mat, row_mat, matched, sums, xh, xl, acc, side):
     pad = jnp.zeros((WIN_PAD - WIN, LANES), f32)
+    side[...] = jnp.zeros_like(side)
+    for h in range(BLOCKS):
+        for i in range(2):
+            row = 2 * h + i
+            row = row + LANES - EDGE if row < EDGE else row - EDGE
+            for q in range(3):
+                side[row : row + 1, q * LANES : (q + 1) * LANES] = win[h, WIN + 3 * i + q : WIN + 3 * i + q + 1]
+    edge = jnp.transpose(side[...])[:WIN]
     for t in range(TILES + 1):
-        x = left[...] if t == 0 else right[...] if t == TILES else win[t - 1]
+        x = edge if t in (0, TILES) else win[t - 1, :WIN]
         xh[t], xl[t] = split(jnp.concatenate([x, pad], 0))
     acc[...] = jnp.zeros_like(acc)
     lane = lax.broadcasted_iota(jnp.int32, (8, LANES), 1)
@@ -158,47 +195,50 @@
                     for s, t in enumerate(ts):
                         matched[b, t, r * LANES : (r + 1) * LANES] = m[i * LANES : (i + 1) * LANES, s * LANES : (s + 1) * LANES]
 
-    def gram(t, keep):
+    def gram(tiles):
         parts = [acc[k] for k in range(26)]
-        for i in range(ROWS // 8):
-            rows = slice(i * 8, i * 8 + 8)
-            m = [matched[b, t, rows] for b in range(BASIS)]
-            d = sci[t, rows]
-            if keep is not None:
-                m = [jnp.where(keep, x, 0.0) for x in m]
-                d = jnp.where(keep, d, 0.0)
-            k = 0
-            for b in range(BASIS):
-                for c in range(b, BASIS):
-                    parts[k] = parts[k] + m[b] * m[c]
-                    k += 1
-            for b in range(BASIS):
-                parts[15 + b] = parts[15 + b] + m[b]
-                parts[20 + b] = parts[20 + b] + m[b] * d
-            parts[25] = parts[25] + d
+        for tile in tiles:
+            for i in range(ROWS // 8):
+                rows = slice(i * 8, i * 8 + 8)
+                if isinstance(tile, tuple):
+                    m = [jnp.where(lane >= HALF, matched[b, tile[0], rows], matched[b, tile[1], rows]) for b in range(BASIS)]
+                    d = jnp.where(lane >= HALF, sci[tile[0], rows], sci[tile[1], rows])
+                else:
+                    m = [matched[b, tile, rows] for b in range(BASIS)]
+                    d = sci[tile, rows]
+                k = 0
+                for b in range(BASIS):
+                    for c in range(b, BASIS):
+                        parts[k] = parts[k] + m[b] * m[c]
+                        k += 1
+                for b in range(BASIS):
+                    parts[15 + b] = parts[15 + b] + m[b]
+                    parts[20 + b] = parts[20 + b] + m[b] * d
+                parts[25] = parts[25] + d
         for k in range(26):
             acc[k] = parts[k]
 
+    rows_of((1, 2))
+
     def pair(p, carry):
-        rows_of((2 * p, 2 * p + 1))
-
-        @pl.when(p > 0)
-        def _():
-            gram(2 * p, None)
-
-        @pl.when(p == 0)
-        def _():
-            gram(0, lane >= HALF)
-
-        gram(2 * p + 1, None)
+        gram((2 * p - 1, 2 * p))
+        rows_of((2 * p + 1, 2 * p + 2))
         return carry
 
-    lax.fori_loop(0, TILES // 2, pair, 0)
-    rows_of((TILES - 1,))
-    gram(TILES - 1, lane < HALF)
+    lax.fori_loop(1, PAIRS, pair, 0)
+    gram((TILES - 4, TILES - 3))
+    rows_of((0, TILES - 1))
+    gram(((0, TILES - 1),))
+    rows_of((TILES - 2,))
+    gram((TILES - 2,))
     rows = [jnp.sum(acc[k], axis=0, keepdims=True) for k in range(26)]
     rows = jnp.concatenate(rows + [jnp.zeros((NSUMS - 26, LANES), f32)], 0)
-    sums[...] = jnp.broadcast_to(jnp.sum(rows, axis=1, keepdims=True), (NSUMS, LANES))
+    total = jnp.broadcast_to(jnp.sum(rows, axis=1, keepdims=True), (NSUMS, LANES))
+    packed = total[:8]
+    for q in range(1, 4):
+        packed = jnp.where(lane >= 32 * q, total[8 * q : 8 * q + 8], packed)
+    for g in range(sums.shape[0]):
+        sums[g] = packed
 
 
 def solve(total, counted):
@@ -234,8 +274,10 @@
     return out
 
 
-def finish_kernel(counted, groups, mine, other, matched, sci, fcol_mat, frow_mat, diff, sig, coef, dh, dl, eh, el, keep):
-    c = solve(mine[...] + other[...], counted)
+def finish_kernel(counted, groups, sums, matched, sci, fcol_mat, frow_mat, diff, sig, coef, eh, el, keep, dout, sout, sems):
+    packed = jnp.sum(sums[...], axis=0)
+    spread = [jnp.broadcast_to(packed[:, 32 * q : 32 * q + 1], (8, LANES)) for q in range(4)]
+    c = solve(jnp.concatenate(spread, 0), counted)
     lane = lax.broadcasted_iota(jnp.int32, (1, LANES), 1)
     coef_row = c[0]
     for b in range(1, BASIS + 1):
@@ -244,28 +286,22 @@
     g = lax.axis_index(GRP[0]) * lax.axis_size(GRP[1]) + lax.axis_index(GRP[1])
     low_ok = jnp.where(g > 0, 1.0, 0.0).astype(f32)
     high_ok = jnp.where(g < groups - 1, 1.0, 0.0).astype(f32)
-    low_mask = jnp.where(lane >= HALF, 1.0, low_ok)
-    high_mask = jnp.where(lane < HALF, 1.0, high_ok)
-
-    def one(t, power):
-        d = sci[t] - c[BASIS]
+
+    def squares(d):
+        return jnp.sum((d * d).reshape(ROWS // 8, 8, LANES), axis=0)
+
+    def residual(t):
         total = c[0] * matched[0, t]
         for b in range(1, BASIS):
             total = total + c[b] * matched[b, t]
-        d = d - total
-        d = d * jnp.where(t == 0, low_mask, jnp.where(t == TILES - 1, high_mask, 1.0))
+        d = sci[t] - total - c[BASIS]
         keep[t] = d
-        dh[t], dl[t] = split(d)
-        own = jnp.where((t == 0) & (lane < HALF), 0.0, jnp.where((t == TILES - 1) & (lane >= HALF), 0.0, 1.0))
-        return power + jnp.sum((d * d * own).reshape(ROWS // 8, 8, LANES), axis=0)
-
-    power = lax.fori_loop(0, TILES, one, jnp.zeros((8, LANES), f32))
-    noise = jnp.sum(jnp.sum(power, axis=0, keepdims=True), axis=1, keepdims=True) / float(ROWS * COLS)
-    scale = 1.0 / jnp.sqrt(jnp.broadcast_to(noise, (1, LANES)) + epsilon)
-
-    def along_rows(ts):
-        d_hi = jnp.concatenate([dh[t] for t in ts], 1)
-        d_lo = jnp.concatenate([dl[t] for t in ts], 1)
+        return d
+
+    def along_rows(ts, ds):
+        halves = [split(d) for d in ds]
+        d_hi = jnp.concatenate([x[0] for x in halves], 1)
+        d_lo = jnp.concatenate([x[1] for x in halves], 1)
         for r in range(2):
             part = slice(0, FBAND) if r == 0 else slice(ROWS - FBAND, ROWS)
             rhs = jnp.concatenate([d_hi[part], d_hi[part], d_lo[part]], 0)
@@ -275,29 +311,50 @@
                 eh[t, r * LANES : (r + 1) * LANES] = e_hi[:, s * LANES : (s + 1) * LANES]
                 el[t, r * LANES : (r + 1) * LANES] = e_lo[:, s * LANES : (s + 1) * LANES]
 
-    def rows_pair(p, carry):
-        along_rows((2 * p, 2 * p + 1))
-        return carry
-
-    lax.fori_loop(0, TILES // 2, rows_pair, 0)
-    along_rows((TILES - 1,))
-    for j in range(BLOCKS):
-        e_hi = jnp.concatenate([eh[j], eh[j + 1]], 1)
-        e_lo = jnp.concatenate([el[j], el[j + 1]], 1)
-        s = jnp.dot(jnp.concatenate([e_hi, e_lo, e_hi], 1), fcol_mat[...], preferred_element_type=f32)
-        sig[:, j * LANES : (j + 1) * LANES] = s * scale
-        diff[:, j * LANES : (j + 1) * LANES] = jnp.concatenate([keep[j][:, HALF:], keep[j + 1][:, :HALF]], 1)
-
-
-def call(kernel, ins, outs, scratch=(), mib=48, flops=0, nbytes=0):
+    def pair(p, power):
+        ts = (2 * p + 1, 2 * p + 2)
+        ds = [residual(t) for t in ts]
+        along_rows(ts, ds)
+        return power + squares(ds[0]) + squares(ds[1])
+
+    power = lax.fori_loop(0, PAIRS, pair, jnp.zeros((8, LANES), f32))
+    last = residual(TILES - 2)
+    along_rows((TILES - 2,), [last])
+    low, high = residual(0), residual(TILES - 1)
+    power = power + squares(last) + squares(jnp.where(lane >= HALF, low, high))
+    low = low * jnp.where(lane >= HALF, 1.0, low_ok)
+    high = high * jnp.where(lane < HALF, 1.0, high_ok)
+    along_rows((0, TILES - 1), [low, high])
+    noise = jnp.sum(jnp.sum(power, axis=0, keepdims=True), axis=1, keepdims=True) / float(ROWS * COLS)
+    scale = 1.0 / jnp.sqrt(jnp.broadcast_to(noise, (1, LANES)) + epsilon)
+
+    copies = []
+    for q in range(PARTS):
+        part = slice(q * COLS // PARTS, (q + 1) * COLS // PARTS)
+        for j in range(q * BLOCKS // PARTS, (q + 1) * BLOCKS // PARTS):
+            e_hi = jnp.concatenate([eh[j], eh[j + 1]], 1)
+            e_lo = jnp.concatenate([el[j], el[j + 1]], 1)
+            s = jnp.dot(jnp.concatenate([e_hi, e_lo, e_hi], 1), fcol_mat[...], preferred_element_type=f32)
+            sout[:, j * LANES : (j + 1) * LANES] = s * scale
+            dout[:, j * LANES : (j + 1) * LANES] = jnp.concatenate([keep[j][:, HALF:], keep[j + 1][:, :HALF]], 1)
+        copies.append(pltpu.make_async_copy(sout.at[:, part], sig.at[:, part], sems.at[2 * q]))
+        copies.append(pltpu.make_async_copy(dout.at[:, part], diff.at[:, part], sems.at[2 * q + 1]))
+        copies[-1].start()
+        copies[-2].start()
+    for copy in copies:
+        copy.wait()
+
+
+def call(kernel, ins, outs, scratch=(), mib=8, flops=0, nbytes=0, out_specs=None, **more):
     return pl.pallas_call(
         kernel,
         out_shape=outs,
         in_specs=ins,
-        out_specs=jax.tree.map(lambda _: VMEM, outs),
+        out_specs=jax.tree.map(lambda _: VMEM, outs) if out_specs is None else out_specs,
         scratch_shapes=list(scratch),
         compiler_params=params(mib),
         cost_estimate=pl.CostEstimate(flops=flops, bytes_accessed=nbytes, transcendentals=0),
+        **more,
     )
 
 
@@ -313,37 +370,53 @@
 def shards(coadd, science, correlation, offset):
     groups = lax.axis_size(GRP)
     up, down = line(groups)
-    sent = call(pack_kernel, [SMEM, SMEM, VMEM], shape(BLOCKS, SENT, LANES), nbytes=4 << 20)(correlation, offset, coadd)
+    first = pl.BlockSpec((ROWS, LANES), lambda i: (0, 0))
+    last = pl.BlockSpec((ROWS, LANES), lambda i: (0, BLOCKS - 1))
+    whole = pl.BlockSpec((2 * EDGE, ROWS), lambda i: (0, 0))
+    to_left, to_right = call(
+        edge_kernel, [first, last, first, last], (shape(2 * EDGE, ROWS),) * 2, out_specs=[whole, whole], grid=(1,)
+    )(coadd, coadd, science, science)
+    from_left = lax.ppermute(to_right, GRP, up)
+    from_right = lax.ppermute(to_left, GRP, down)
+    sent = call(pack_kernel, [SMEM, SMEM, VMEM, VMEM, VMEM], shape(BLOCKS, SENT, LANES), nbytes=4 << 20)(
+        correlation, offset, coadd, from_left, from_right
+    )
     held = lax.all_to_all(sent, "visit", 0, 0, tiled=True)
-    sci_left = lax.ppermute(science[:, COLS - LANES :], GRP, up)
-    sci_right = lax.ppermute(science[:, :LANES], GRP, down)
-    framed = call(frame_kernel, [VMEM] * 3, shape(TILES, ROWS, LANES), nbytes=4 << 20)(science, sci_left, sci_right)
-    meta = held[:, ROWS, :2].astype(jnp.int32)
+    framed = call(
+        frame_kernel, [VMEM] * 3, shape(TILES, ROWS, LANES), [pltpu.VMEM((LANES, ROWS), f32)], nbytes=4 << 20
+    )(science, from_left, from_right)
+    meta = held[:, ROWS + 4, :2].astype(jnp.int32)
     picked = call(
-        pick_kernel, [SMEM, VMEM], shape(BLOCKS, WIN, LANES), [pltpu.VMEM((STRIP + ROWS + 8, LANES), f32)], nbytes=5 << 20
+        pick_kernel,
+        [SMEM, VMEM],
+        shape(BLOCKS, WIN + 8, LANES),
+        [pltpu.VMEM((STRIP + ROWS + 8, LANES), f32), pltpu.VMEM((8, STRIP + 2 * ROWS), f32)],
+        nbytes=5 << 20,
     )(meta, held)
     win = lax.all_to_all(picked, "visit", 0, 0, tiled=True)
-    left = lax.ppermute(win[BLOCKS - 1], GRP, up)
-    right = lax.ppermute(win[0], GRP, down)
     tile16 = pltpu.VMEM((TILES + 1, WIN_PAD, LANES), bf16)
     matched, sums = call(
         match_kernel,
-        [VMEM] * 6,
-        (shape(BASIS, TILES, ROWS, LANES), shape(NSUMS, LANES)),
-        [tile16, tile16, pltpu.VMEM((26, 8, LANES), f32)],
+        [VMEM] * 4,
+        (shape(BASIS, TILES, ROWS, LANES), shape(groups, 8, LANES)),
+        [tile16, tile16, pltpu.VMEM((26, 8, LANES), f32), pltpu.VMEM((LANES, 3 * LANES), f32)],
         flops=8 << 30,
-    )(win, left, right, framed, jnp.asarray(COL_MAT), jnp.asarray(ROW_MAT))
-    for axis, swap in ((GRP[1], [(0, 1), (1, 0)]), (GRP[0], [(0, 1), (1, 0), (2, 3), (3, 2)])):
-        sums = sums + lax.ppermute(sums, axis, swap)
-    other = lax.ppermute(sums, GRP[0], [(0, 3), (3, 0), (1, 2), (2, 1)])
+        mib=12,
+    )(win, framed, jnp.asarray(COL_MAT), jnp.asarray(ROW_MAT))
+    sums = lax.all_to_all(sums, GRP, 0, 0, tiled=True)
     block16 = pltpu.VMEM((TILES, ROWS, LANES), bf16)
+    image = pltpu.VMEM((ROWS, COLS), f32)
+    anywhere = pl.BlockSpec(memory_space=pl.ANY)
     return call(
         functools.partial(finish_kernel, float(ROWS * COLS * groups), groups),
-        [VMEM] * 6,
+        [VMEM] * 5,
         (shape(ROWS, COLS), shape(ROWS, COLS), shape(1, BASIS + 1)),
-        [block16] * 4 + [pltpu.VMEM((TILES, ROWS, LANES), f32)],
+        [block16] * 2
+        + [pltpu.VMEM((TILES, ROWS, LANES), f32), image, image, pltpu.SemaphoreType.DMA((2 * PARTS,))],
         flops=3 << 30,
-    )(sums, other, matched, framed, jnp.asarray(FCOL_MAT), jnp.asarray(FROW_MAT))
+        mib=16,
+        out_specs=(anywhere, anywhere, VMEM),
+    )(sums, matched, framed, jnp.asarray(FCOL_MAT), jnp.asarray(FROW_MAT))
 
 
 def solution(mesh):

time: 143 us -> 126 us (0.88)
  waiting for transfers between devices: 8.79 us -> 32.8 us
  blocking collectives: 67.3 us -> 48.4 us
  starting transfers between devices: 27.4 us -> 11.2 us
  Pallas kernels: 34.6 us -> 22.1 us
  local copies, waits for them, and re-layouts: 1.66 us -> 8.71 us
    all_to_all x0 -> x1, waiting for transfers between devices: none -> 28.1 us  [shards(): win = lax.all_to_all(picked, 'visit', 0, 0, tiled=True)]
    ppermute x7 -> x2, starting transfers between devices: 27.4 us -> 6.61 us  [the longest x1 5.31 us: shards(): from_left = lax.ppermute(to_right, GRP, up)]
    all_to_all x1, blocking collectives: 32.6 us -> 14.6 us  [shards(): sums = lax.all_to_all(sums, GRP, 0, 0, tiled=True)]
    pallas_call x4 -> x5, Pallas kernels: 23.2 us -> 16 us  [the longest x1 12.1 us: shards(): call(match_kernel, [VMEM] * 4, (shape(BASIS, TILES, ROWS, LANES), shape(g...]
    unnamed x14 -> x22, local copies, waits for them, and re-layouts: 1.62 us -> 8.71 us
    pallas_call x1, Pallas kernels: 11.5 us -> 6.17 us  [shards(): call(functools.partial(finish_kernel, float(ROWS * COLS * groups), groups...]
    all_to_all x0 -> x1, starting transfers between devices: none -> 4.58 us  [shards(): win = lax.all_to_all(picked, 'visit', 0, 0, tiled=True)]
    ppermute x7 -> x2, waiting for transfers between devices: 8.79 us -> 4.71 us  [the longest x1 4.71 us: shards(): from_right = lax.ppermute(to_left, GRP, down)]
  transfers between devices with their start and end apart: 7 -> 3, of which waited for: 5 -> 2; matrix products, arithmetic and copies ran while one was open for 0% -> 0% of each run, Pallas kernels for 1% -> 1%
where the time goes in v2:
time: 126 us; the launch traced here: 125 us
  blocking collectives  48.4 us (38%)
  waiting for transfers between devices  32.8 us (26%)
  Pallas kernels  22.1 us (18%)
  starting transfers between devices  11.2 us (9%)
  local copies, waits for them, and re-layouts  8.71 us (7%)
  between operations  2.04 us (2%)
    all_to_all x1, blocking collectives, shards(): held = lax.all_to_all(sent, 'visit', 0, 0, tiled=True)  33.8 us
    all_to_all x1, waiting for transfers between devices, shards(): win = lax.all_to_all(picked, 'visit', 0, 0, tiled=True)  28.1 us
    all_to_all x1, blocking collectives, shards(): sums = lax.all_to_all(sums, GRP, 0, 0, tiled=True)  14.6 us
    pallas_call x1, Pallas kernels, shards(): call(match_kernel, [VMEM] * 4, (shape(BASIS, TILES, ROWS, LANES), shape(g...  12.1 us
    unnamed x22, local copies, waits for them, and re-layouts  8.71 us
    pallas_call x1, Pallas kernels, shards(): call(functools.partial(finish_kernel, float(ROWS * COLS * groups), groups...  6.17 us
    ppermute x1, starting transfers between devices, shards(): from_left = lax.ppermute(to_right, GRP, up)  5.31 us
    ppermute x1, waiting for transfers between devices, shards(): from_right = lax.ppermute(to_left, GRP, down)  4.71 us
  transfers between devices with their start and end apart: 3, of which 2 were waited for; matrix products, arithmetic and copies ran while one was open for 0% of the time, Pallas kernels for 1%

profile of v2, /device:TPU:0, one launch (start us, length us, event | category | flops | bytes accessed | tf_op | source)
XLA Modules:
  0.0 125.2 jit_solution(9031930117507143614)
XLA Ops:
  0.6 0.0 copy-start
  0.6 1.6 %copy-done = f32[256,2048]{1,0:T(8,128)S(1)} copy-done((f32[256,2048]{1,0:T(8,128)S(1)}, f32[256,2048]{1,0:T(8,128)}, u32[]{:S(2)}) %copy-start) | copy-done | bytes 2097176
  2.2 0.0 copy-start.2
  2.2 1.6 %copy-done.2 = f32[256,2048]{1,0:T(8,128)S(1)} copy-done((f32[256,2048]{1,0:T(8,128)S(1)}, f32[256,2048]{1,0:T(8,128)}, u32[]{:S(2)}) %copy-start.2) | copy-done | bytes 2097176
  3.8 0.0 copy-start.1
  3.8 0.2 shard_map.103
  4.0 5.3 %collective-permute-start = (f32[32,256]{1,0:T(8,128)S(1)}, f32[32,256]{1,0:T(8,128)S(1)}, u32[]{:S(2)}, u32[]{:S(2)}) collective-permute-start(f32[32,256]{1,0:T(8,128)S(1)} %get-tuple-element.7), channel_id=1, source_target_pairs={{0,1},{1,2},{2,3},{3,4},{4,5},{5,6},{6,7},{8,9},{9,10},{10,11},{11... | collective-permute-start | bytes 98312 | tf_op jit(solution)/shard_map/ppermute | solution.py:379
  9.3 1.3 %collective-permute-start.1 = (f32[32,256]{1,0:T(8,128)S(1)}, f32[32,256]{1,0:T(8,128)S(1)}, u32[]{:S(2)}, u32[]{:S(2)}) collective-permute-start(f32[32,256]{1,0:T(8,128)S(1)} %get-tuple-element.8), channel_id=1, source_target_pairs={{1,0},{2,1},{3,2},{4,3},{5,4},{6,5},{7,6},{9,8},{10,9},{11,10},{12... | collective-permute-start | bytes 98312 | tf_op jit(solution)/shard_map/ppermute | solution.py:380
  11.9 0.0 collective-permute-done.from_left
  11.9 4.7 %collective-permute-done.1.from_right = f32[32,256]{1,0:T(8,128)S(1)} collective-permute-done((f32[32,256]{1,0:T(8,128)S(1)}, f32[32,256]{1,0:T(8,128)S(1)}, u32[]{:S(2)}, u32[]{:S(2)}) %collective-permute-start.1) | collective-permute-done | bytes 32800 | tf_op jit(solution)/shard_map/ppermute | solution.py:380
  16.6 0.0 copy-done.1
  16.7 0.2 shard_map.104
  16.8 33.8 %all_to_all.15.held = f32[16,264,128]{2,1,0:T(8,128)S(1)} all-to-all(f32[16,264,128]{2,1,0:T(8,128)S(1)} %shard_map.104), channel_id=1, replica_groups=mesh['visit'=16,'grp_0'=4,'grp_1'=2] {'visit'}, dimensions={0} | all-to-all | bytes 4325376 | tf_op jit(solution)/shard_map/all_to_all | solution.py:384
  50.6 2.3 %shard_map.105 = f32[16,288,128]{2,1,0:T(8,128)S(1)} custom-call(s32[16,2]{1,0:T(8,128)S(1)} %bitcast.1, f32[16,264,128]{2,1,0:T(8,128)S(1)} %all_to_all.15.held), custom_call_target="tpu_custom_call" | custom-call | bytes 5242880 | tf_op jit(solution)/shard_map/pallas_call | solution.py:389
  52.9 0.0 copy-start.4
  52.9 1.4 %copy-done.4 = f32[16,288,128]{2,1,0:T(8,128)} copy-done((f32[16,288,128]{2,1,0:T(8,128)}, f32[16,288,128]{2,1,0:T(8,128)S(1)}, u32[]{:S(2)}) %copy-start.4) | copy-done | bytes 2359320
  54.3 0.0 copy-start.3
  54.3 4.6 %all-to-all-start.1 = ((f32[16,288,128]{2,1,0:T(8,128)}), f32[16,288,128]{2,1,0:T(8,128)}, u32[]{:S(2)}, u32[]{:S(2)}) async-start(f32[16,288,128]{2,1,0:T(8,128)} %copy-done.4), calls=%async_computation.1 | async-start | bytes 4718592 | tf_op jit(solution)/shard_map/all_to_all | solution.py:396
  58.9 0.0 copy-done.3
  58.9 0.0 copy-start.9
  58.9 1.2 shard_map.106.sci
  60.2 0.0 copy-start.5
  60.2 1.4 %copy-done.5 = f32[17,256,128]{2,1,0:T(8,128)} copy-done((f32[17,256,128]{2,1,0:T(8,128)}, f32[17,256,128]{2,1,0:T(8,128)S(1)}, u32[]{:S(2)}) %copy-start.5) | copy-done | bytes 2228248
  61.6 28.1 %all-to-all-done.1.win = f32[16,288,128]{2,1,0:T(8,128)} async-done(((f32[16,288,128]{2,1,0:T(8,128)}), f32[16,288,128]{2,1,0:T(8,128)}, u32[]{:S(2)}, u32[]{:S(2)}) %all-to-all-start.1) | async-done | bytes 2359328 | tf_op jit(solution)/shard_map/all_to_all | solution.py:396
  89.6 0.0 copy-done.9
  89.6 1.6 %copy-done.6 = f32[17,256,128]{2,1,0:T(8,128)S(1)} copy-done((f32[17,256,128]{2,1,0:T(8,128)S(1)}, f32[17,256,128]{2,1,0:T(8,128)}, u32[]{:S(2)}) %copy-start.6) | copy-done | bytes 2228248
  91.2 1.1 copy-done.10
  92.3 12.1 %shard_map.107 = (f32[5,17,256,128]{3,2,1,0:T(8,128)S(1)}, f32[8,8,128]{2,1,0:T(8,128)S(1)}) custom-call(f32[16,288,128]{2,1,0:T(8,128)} %all-to-all-done.1.win, f32[17,256,128]{2,1,0:T(8,128)S(1)} %copy-done.6, bf16[768,512]{1,0:T(8,128)(2,1)S(1)} %copy-done.9, bf16[640,480]{1,0:T(8,128)(2,1)S(1)} %copy-done.10), custom_call_target="tpu_custom_call" | custom-call | flops 8589934592 | tf_op jit(solution)/shard_map/pallas_call | solution.py:398
  104.5 14.6 %all_to_all.16.sums = f32[8,8,128]{2,1,0:T(8,128)S(1)} all-to-all(f32[8,8,128]{2,1,0:T(8,128)S(1)} %get-tuple-element.9), channel_id=1, replica_groups=mesh['visit'=16,'grp_0'=4,'grp_1'=2] {'grp_0','grp_1'}, dimensions={0} | all-to-all | bytes 65536 | tf_op jit(solution)/shard_map/all_to_all | solution.py:406
  119.1 0.0 copy-done.7
  119.1 0.0 copy-done.8
  119.1 6.2 %shard_map.108 = (f32[256,2048]{1,0:T(8,128)}, f32[256,2048]{1,0:T(8,128)}, f32[1,6]{1,0:T(1,128)}) custom-call(f32[8,8,128]{2,1,0:T(8,128)S(1)} %all_to_all.16.sums, f32[5,17,256,128]{3,2,1,0:T(8,128)S(1)} %get-tuple-element.10.matched, f32[17,256,128]{2,1,0:T(8,128)S(1)} %copy-done.6, bf16[768,128]{1,0:T(8,128)(2,1)S(1)} %copy-done.8, ...), custom_call_target="tpu_custom_call" | custom-call | flops 3221225472 | tf_op jit(solution)/shard_map/pallas_call | solution.py:410
  (5 shorter events, 0.0 us)
Async XLA Ops:
  0.6 1.6 %copy-start = (f32[256,2048]{1,0:T(8,128)S(1)}, f32[256,2048]{1,0:T(8,128)}, u32[]{:S(2)}) copy-start(f32[256,2048]{1,0:T(8,128)} %coadd.1) | copy-start | bytes 6291460
  2.2 1.6 %copy-start.2 = (f32[256,2048]{1,0:T(8,128)S(1)}, f32[256,2048]{1,0:T(8,128)}, u32[]{:S(2)}) copy-start(f32[256,2048]{1,0:T(8,128)} %science.1) | copy-start | bytes 6291460
  3.8 12.8 %copy-start.1 = (f32[256,2048]{1,0:T(8,128)S(1)}, f32[256,2048]{1,0:T(8,128)}, u32[]{:S(2)}) copy-start(f32[256,2048]{1,0:T(8,128)} %coadd.1) | copy-start | bytes 6291460
  4.0 7.9 %collective-permute-start = (f32[32,256]{1,0:T(8,128)S(1)}, f32[32,256]{1,0:T(8,128)S(1)}, u32[]{:S(2)}, u32[]{:S(2)}) collective-permute-start(f32[32,256]{1,0:T(8,128)S(1)} %get-tuple-element.7), channel_id=1, source_target_pairs={{0,1},{1,2},{2,3},{3,4},{4,5},{5,6},{6,7},{8,9},{9,10},{10,11},{11... | collective-permute-start | bytes 98312 | tf_op jit(solution)/shard_map/ppermute | solution.py:379
  9.3 7.3 %collective-permute-start.1 = (f32[32,256]{1,0:T(8,128)S(1)}, f32[32,256]{1,0:T(8,128)S(1)}, u32[]{:S(2)}, u32[]{:S(2)}) collective-permute-start(f32[32,256]{1,0:T(8,128)S(1)} %get-tuple-element.8), channel_id=1, source_target_pairs={{1,0},{2,1},{3,2},{4,3},{5,4},{6,5},{7,6},{9,8},{10,9},{11,10},{12... | collective-permute-start | bytes 98312 | tf_op jit(solution)/shard_map/ppermute | solution.py:380
  52.9 1.4 %copy-start.4 = (f32[16,288,128]{2,1,0:T(8,128)}, f32[16,288,128]{2,1,0:T(8,128)S(1)}, u32[]{:S(2)}) copy-start(f32[16,288,128]{2,1,0:T(8,128)S(1)} %shard_map.105) | copy-start | bytes 7077892
  54.3 4.6 %copy-start.3 = (f32[256,2048]{1,0:T(8,128)S(1)}, f32[256,2048]{1,0:T(8,128)}, u32[]{:S(2)}) copy-start(f32[256,2048]{1,0:T(8,128)} %science.1) | copy-start | bytes 6291460
  54.3 35.3 %all-to-all-start.1 = ((f32[16,288,128]{2,1,0:T(8,128)}), f32[16,288,128]{2,1,0:T(8,128)}, u32[]{:S(2)}, u32[]{:S(2)}) async-start(f32[16,288,128]{2,1,0:T(8,128)} %copy-done.4), calls=%async_computation.1 | async-start | bytes 4718592 | tf_op jit(solution)/shard_map/all_to_all | solution.py:396
  58.9 30.7 %copy-start.9 = (bf16[768,512]{1,0:T(8,128)(2,1)S(1)}, bf16[768,512]{1,0:T(8,128)(2,1)}, u32[]{:S(2)}) copy-start(bf16[768,512]{1,0:T(8,128)(2,1)} %constant.8.clone.col_mat) | copy-start | bytes 2359300
  60.2 1.4 %copy-start.5 = (f32[17,256,128]{2,1,0:T(8,128)}, f32[17,256,128]{2,1,0:T(8,128)S(1)}, u32[]{:S(2)}) copy-start(f32[17,256,128]{2,1,0:T(8,128)S(1)} %shard_map.106.sci) | copy-start | bytes 6684676
  89.6 1.6 %copy-start.6 = (f32[17,256,128]{2,1,0:T(8,128)S(1)}, f32[17,256,128]{2,1,0:T(8,128)}, u32[]{:S(2)}) copy-start(f32[17,256,128]{2,1,0:T(8,128)} %copy-done.5) | copy-start | bytes 6684676
  91.2 1.1 copy-start.10
  92.3 26.7 %copy-start.7 = (bf16[256,432]{1,0:T(8,128)(2,1)S(1)}, bf16[256,432]{1,0:T(8,128)(2,1)}, u32[]{:S(2)}) copy-start(bf16[256,432]{1,0:T(8,128)(2,1)} %constant.11.clone.frow_mat) | copy-start | bytes 663556
  92.3 26.7 %copy-start.8 = (bf16[768,128]{1,0:T(8,128)(2,1)S(1)}, bf16[768,128]{1,0:T(8,128)(2,1)}, u32[]{:S(2)}) copy-start(bf16[768,128]{1,0:T(8,128)(2,1)} %constant.10.clone.fcol_mat) | copy-start | bytes 589828

commit v3 on v2

--- a/solution.py
+++ b/solution.py
@@ -105,15 +105,22 @@
     to_right[EDGE:] = jnp.transpose(sci_last[...])[LANES - EDGE :]
 
 
-def pack_kernel(tile_id, shift, coadd, from_left, from_right, out):
-    lane = lax.broadcasted_iota(jnp.int32, (4, LANES), 1)
+def pack_kernel(tile_id, shift, coadd, out):
+    lane = lax.broadcasted_iota(jnp.int32, (8, LANES), 1)
     meta = jnp.where(lane == 0, tile_id[0].astype(f32), shift[0].astype(f32))
     for h in range(BLOCKS):
         out[h, :ROWS] = coadd[:, h * LANES : (h + 1) * LANES]
+        out[h, ROWS:] = meta
+
+
+def patch_kernel(packed, from_left, from_right, out):
+    for h in range(BLOCKS):
         source = from_left if h < BLOCKS // 2 else from_right
         k = 2 * h % EDGE
-        pieces = [source[k + i : k + i + 1, q * LANES : (q + 1) * LANES] for i in range(2) for q in range(2)]
-        out[h, ROWS:] = jnp.concatenate(pieces + [meta], 0)
+        for i in range(2):
+            for q in range(2):
+                row = ROWS + 2 * i + q
+                out[h, row : row + 1] = source[k + i : k + i + 1, q * LANES : (q + 1) * LANES]
 
 
 def pick_kernel(meta, held, out, strip, edges):
@@ -145,20 +152,7 @@
     lax.fori_loop(0, BLOCKS, one, 0)
 
 
-def frame_kernel(science, from_left, from_right, out, side):
-    side[...] = jnp.zeros_like(side)
-    side[:EDGE] = from_right[EDGE:]
-    side[LANES - EDGE :] = from_left[EDGE:]
-    edge = jnp.transpose(side[...])
-
-    def block(t):
-        return edge if t in (-1, BLOCKS) else science[:, t * LANES : (t + 1) * LANES]
-
-    for t in range(TILES):
-        out[t] = jnp.concatenate([block(t - 1)[:, HALF:], block(t)[:, :HALF]], 1)
-
-
-def match_kernel(win, sci, col_mat, row_mat, matched, sums, xh, xl, acc, side):
+def match_kernel(win, science, from_left, from_right, col_mat, row_mat, matched, sci, sums, xh, xl, acc, side):
     pad = jnp.zeros((WIN_PAD - WIN, LANES), f32)
     side[...] = jnp.zeros_like(side)
     for h in range(BLOCKS):
@@ -171,6 +165,12 @@
     for t in range(TILES + 1):
         x = edge if t in (0, TILES) else win[t - 1, :WIN]
         xh[t], xl[t] = split(jnp.concatenate([x, pad], 0))
+    side[:, :ROWS] = jnp.zeros((LANES, ROWS), f32)
+    side[:EDGE, :ROWS] = from_right[EDGE:]
+    side[LANES - EDGE :, :ROWS] = from_left[EDGE:]
+    sci_edge = jnp.transpose(side[:, :ROWS])
+    sci[0] = jnp.concatenate([sci_edge[:, HALF:], science[:, :HALF]], 1)
+    sci[TILES - 1] = jnp.concatenate([science[:, COLS - HALF :], sci_edge[:, :HALF]], 1)
     acc[...] = jnp.zeros_like(acc)
     lane = lax.broadcasted_iota(jnp.int32, (8, LANES), 1)
 
@@ -180,7 +180,17 @@
         y = jnp.dot(jnp.concatenate([a_hi, a_lo, a_hi], 1), col_mat[...], preferred_element_type=f32)
         return split(y)
 
+    def frame(t):
+        at = (t - 1) * LANES
+        if not isinstance(t, int):
+            at = pl.multiple_of(at, LANES)
+        wide = science[:, pl.ds(at, 2 * LANES)]
+        sci[t] = jnp.concatenate([wide[:, HALF:LANES], wide[:, LANES : LANES + HALF]], 1)
+
     def rows_of(ts):
+        for t in ts:
+            if not isinstance(t, int) or 0 < t < TILES - 1:
+                frame(t)
         ys = [layers(t) for t in ts]
         for f, bases in enumerate(((0,), (1, 3), (2,), (4,))):
             lo = (0, 1, 3, 4)[f] * LANES
@@ -370,21 +380,20 @@
 def shards(coadd, science, correlation, offset):
     groups = lax.axis_size(GRP)
     up, down = line(groups)
-    first = pl.BlockSpec((ROWS, LANES), lambda i: (0, 0))
-    last = pl.BlockSpec((ROWS, LANES), lambda i: (0, BLOCKS - 1))
-    whole = pl.BlockSpec((2 * EDGE, ROWS), lambda i: (0, 0))
-    to_left, to_right = call(
-        edge_kernel, [first, last, first, last], (shape(2 * EDGE, ROWS),) * 2, out_specs=[whole, whole], grid=(1,)
-    )(coadd, coadd, science, science)
+    mats = [jnp.asarray(m) for m in (COL_MAT, ROW_MAT, FCOL_MAT, FROW_MAT)]
+    to_left, to_right = call(edge_kernel, [VMEM] * 4, (shape(2 * EDGE, ROWS),) * 2)(
+        coadd[:, :LANES], coadd[:, COLS - LANES :], science[:, :LANES], science[:, COLS - LANES :]
+    )
     from_left = lax.ppermute(to_right, GRP, up)
     from_right = lax.ppermute(to_left, GRP, down)
-    sent = call(pack_kernel, [SMEM, SMEM, VMEM, VMEM, VMEM], shape(BLOCKS, SENT, LANES), nbytes=4 << 20)(
-        correlation, offset, coadd, from_left, from_right
+    coadd, _, _ = lax.optimization_barrier((coadd, to_left, to_right))
+    packed = call(pack_kernel, [SMEM, SMEM, VMEM], shape(BLOCKS, SENT, LANES), flops=1 << 20, nbytes=4 << 20)(
+        correlation, offset, coadd
+    )
+    sent = call(patch_kernel, [VMEM] * 3, shape(BLOCKS, SENT, LANES), input_output_aliases={0: 0})(
+        packed, from_left, from_right
     )
     held = lax.all_to_all(sent, "visit", 0, 0, tiled=True)
-    framed = call(
-        frame_kernel, [VMEM] * 3, shape(TILES, ROWS, LANES), [pltpu.VMEM((LANES, ROWS), f32)], nbytes=4 << 20
-    )(science, from_left, from_right)
     meta = held[:, ROWS + 4, :2].astype(jnp.int32)
     picked = call(
         pick_kernel,
@@ -395,14 +404,14 @@
     )(meta, held)
     win = lax.all_to_all(picked, "visit", 0, 0, tiled=True)
     tile16 = pltpu.VMEM((TILES + 1, WIN_PAD, LANES), bf16)
-    matched, sums = call(
+    matched, framed, sums = call(
         match_kernel,
-        [VMEM] * 4,
-        (shape(BASIS, TILES, ROWS, LANES), shape(groups, 8, LANES)),
+        [VMEM] * 6,
+        (shape(BASIS, TILES, ROWS, LANES), shape(TILES, ROWS, LANES), shape(groups, 8, LANES)),
         [tile16, tile16, pltpu.VMEM((26, 8, LANES), f32), pltpu.VMEM((LANES, 3 * LANES), f32)],
         flops=8 << 30,
         mib=12,
-    )(win, framed, jnp.asarray(COL_MAT), jnp.asarray(ROW_MAT))
+    )(win, science, from_left, from_right, *mats[:2])
     sums = lax.all_to_all(sums, GRP, 0, 0, tiled=True)
     block16 = pltpu.VMEM((TILES, ROWS, LANES), bf16)
     image = pltpu.VMEM((ROWS, COLS), f32)
@@ -416,7 +425,7 @@
         flops=3 << 30,
         mib=16,
         out_specs=(anywhere, anywhere, VMEM),
-    )(sums, matched, framed, jnp.asarray(FCOL_MAT), jnp.asarray(FROW_MAT))
+    )(sums, matched, framed, *mats[2:])
 
 
 def solution(mesh):

time: 126 us -> 116 us (0.921)
  blocking collectives: 48.4 us -> 83.2 us
  waiting for transfers between devices: 32.8 us -> 0.01 us
  local copies, waits for them, and re-layouts: 8.71 us -> 2.76 us
  starting transfers between devices: 11.2 us -> 7.34 us
  Pallas kernels: 22.1 us -> 20.8 us
    all_to_all x0 -> x1, blocking collectives: none -> 33.4 us  [shards(): win = lax.all_to_all(picked, 'visit', 0, 0, tiled=True)]
    all_to_all x1 -> x0, waiting for transfers between devices: 28.1 us -> none  [shards(): win = lax.all_to_all(picked, 'visit', 0, 0, tiled=True)]
    unnamed x22 -> x12, local copies, waits for them, and re-layouts: 8.71 us -> 1.62 us
    ppermute x1, waiting for transfers between devices: 4.71 us -> 0.01 us  [shards(): from_right = lax.ppermute(to_left, GRP, down)]
    all_to_all x1 -> x0, starting transfers between devices: 4.58 us -> none  [shards(): win = lax.all_to_all(picked, 'visit', 0, 0, tiled=True)]
    pallas_call x4, Pallas kernels: 13.7 us -> 12.3 us  [the longest x1 12 us: shards(): call(match_kernel, [VMEM] * 6, (shape(BASIS, TILES, ROWS, LANES), shape(T...]
  transfers between devices with their start and end apart: 3 -> 2, of which waited for: 2 -> 0; matrix products, arithmetic and copies ran while one was open for 0% -> 0% of each run, Pallas kernels for 1% -> 0%
where the time goes in v3:
time: 116 us
  blocking collectives  83.2 us (72%)
  Pallas kernels  20.8 us (18%)
  starting transfers between devices  7.34 us (6%)
  local copies, waits for them, and re-layouts  2.76 us (2%)
  between operations  2.05 us (2%)
    all_to_all x1, blocking collectives, shards(): held = lax.all_to_all(sent, 'visit', 0, 0, tiled=True)  34.8 us
    all_to_all x1, blocking collectives, shards(): win = lax.all_to_all(picked, 'visit', 0, 0, tiled=True)  33.4 us
    all_to_all x1, blocking collectives, shards(): sums = lax.all_to_all(sums, GRP, 0, 0, tiled=True)  15 us
    pallas_call x1, Pallas kernels, shards(): call(match_kernel, [VMEM] * 6, (shape(BASIS, TILES, ROWS, LANES), shape(T...  12 us
    pallas_call x1, Pallas kernels, shards(): call(functools.partial(finish_kernel, float(ROWS * COLS * groups), groups...  6.17 us
    ppermute x1, starting transfers between devices, shards(): from_left = lax.ppermute(to_right, GRP, up)  6.05 us
  transfers between devices with their start and end apart: 2, of which 0 were waited for; matrix products, arithmetic and copies ran while one was open for 0% of the time, Pallas kernels for 0%

profile of v3, /device:TPU:0, one launch (start us, length us, event | category | flops | bytes accessed | tf_op | source)
XLA Modules:
  0.0 116.2 jit_solution(970539210651637555)
XLA Ops:
  0.6 1.1 fusion
  1.8 0.2 shard_map.103
  2.0 1.3 %collective-permute-start.1 = (f32[32,256]{1,0:T(8,128)S(1)}, f32[32,256]{1,0:T(8,128)S(1)}, u32[]{:S(2)}, u32[]{:S(2)}) collective-permute-start(f32[32,256]{1,0:T(8,128)S(1)} %get-tuple-element.9), channel_id=1, source_target_pairs={{1,0},{2,1},{3,2},{4,3},{5,4},{6,5},{7,6},{9,8},{10,9},{11,10},{12... | collective-permute-start | bytes 98312 | tf_op jit(solution)/shard_map/ppermute | solution.py:388
  3.3 6.1 %collective-permute-start = (f32[32,256]{1,0:T(8,128)S(1)}, f32[32,256]{1,0:T(8,128)S(1)}, u32[]{:S(2)}, u32[]{:S(2)}) collective-permute-start(f32[32,256]{1,0:T(8,128)S(1)} %get-tuple-element.10), channel_id=1, source_target_pairs={{0,1},{1,2},{2,3},{3,4},{4,5},{5,6},{6,7},{8,9},{9,10},{10,11},{11... | collective-permute-start | bytes 98312 | tf_op jit(solution)/shard_map/ppermute | solution.py:387
  10.6 0.0 copy-start
  10.6 1.6 %copy-done = f32[256,2048]{1,0:T(8,128)S(1)} copy-done((f32[256,2048]{1,0:T(8,128)S(1)}, f32[256,2048]{1,0:T(8,128)}, u32[]{:S(2)}) %copy-start) | copy-done | bytes 2097176
  12.2 0.2 shard_map.104.packed
  12.4 0.0 collective-permute-done.1.from_right
  12.4 0.0 collective-permute-done.from_left
  12.4 34.8 %all_to_all.15.held = f32[16,264,128]{2,1,0:T(8,128)S(1)} all-to-all(f32[16,264,128]{2,1,0:T(8,128)S(1)} %shard_map.105), channel_id=1, replica_groups=mesh['visit'=16,'grp_0'=4,'grp_1'=2] {'visit'}, dimensions={0} | all-to-all | bytes 4325376 | tf_op jit(solution)/shard_map/all_to_all | solution.py:396
  47.2 2.3 %shard_map.106 = f32[16,288,128]{2,1,0:T(8,128)S(1)} custom-call(s32[16,2]{1,0:T(8,128)S(1)} %bitcast.1, f32[16,264,128]{2,1,0:T(8,128)S(1)} %all_to_all.15.held), custom_call_target="tpu_custom_call" | custom-call | bytes 5242880 | tf_op jit(solution)/shard_map/pallas_call | solution.py:398
  49.5 0.0 copy-start.3
  49.5 0.0 copy-start.4
  49.5 0.0 copy-start.5
  49.5 33.4 %all_to_all.16.win = f32[16,288,128]{2,1,0:T(8,128)S(1)} all-to-all(f32[16,288,128]{2,1,0:T(8,128)S(1)} %shard_map.106), channel_id=1, replica_groups=mesh['visit'=16,'grp_0'=4,'grp_1'=2] {'visit'}, dimensions={0} | all-to-all | bytes 4718592 | tf_op jit(solution)/shard_map/all_to_all | solution.py:405
  82.9 0.0 copy-done.3
  82.9 0.0 copy-done.4
  82.9 0.0 copy-done.5
  83.0 0.0 copy-start.1
  83.0 0.0 copy-start.2
  83.0 12.0 %shard_map.107 = (f32[5,17,256,128]{3,2,1,0:T(8,128)S(1)}, f32[17,256,128]{2,1,0:T(8,128)S(1)}, f32[8,8,128]{2,1,0:T(8,128)S(1)}) custom-call(f32[16,288,128]{2,1,0:T(8,128)S(1)} %all_to_all.16.win, f32[256,2048]{1,0:T(8,128)S(1)} %copy-done.3, f32[32,256]{1,0:T(8,128)S(1)} %collective-permute-done.from_left, ...), custom_call_target="tpu_custom_call" | custom-call | flops 8589934592 | tf_op jit(solution)/shard_map/pallas_call | solution.py:407
  94.9 15.0 %all_to_all.17.sums = f32[8,8,128]{2,1,0:T(8,128)S(1)} all-to-all(f32[8,8,128]{2,1,0:T(8,128)S(1)} %get-tuple-element.12), channel_id=1, replica_groups=mesh['visit'=16,'grp_0'=4,'grp_1'=2] {'grp_0','grp_1'}, dimensions={0} | all-to-all | bytes 65536 | tf_op jit(solution)/shard_map/all_to_all | solution.py:415
  110.0 0.0 copy-done.1
  110.0 0.0 copy-done.2
  110.0 6.2 %shard_map.108 = (f32[256,2048]{1,0:T(8,128)}, f32[256,2048]{1,0:T(8,128)}, f32[1,6]{1,0:T(1,128)}) custom-call(f32[8,8,128]{2,1,0:T(8,128)S(1)} %all_to_all.17.sums, f32[5,17,256,128]{3,2,1,0:T(8,128)S(1)} %get-tuple-element.13.matched, f32[17,256,128]{2,1,0:T(8,128)S(1)} %get-tuple-element.14.sci, bf16[768,128]{1,0:T(8,128)(2,1)S(1)} %copy-done.2, ...), custom_call_target="tpu_custom_call" | custom-call | flops 3221225472 | tf_op jit(solution)/shard_map/pallas_call | solution.py:419
  (2 shorter events, 0.0 us)
Async XLA Ops:
  2.0 10.4 %collective-permute-start.1 = (f32[32,256]{1,0:T(8,128)S(1)}, f32[32,256]{1,0:T(8,128)S(1)}, u32[]{:S(2)}, u32[]{:S(2)}) collective-permute-start(f32[32,256]{1,0:T(8,128)S(1)} %get-tuple-element.9), channel_id=1, source_target_pairs={{1,0},{2,1},{3,2},{4,3},{5,4},{6,5},{7,6},{9,8},{10,9},{11,10},{12... | collective-permute-start | bytes 98312 | tf_op jit(solution)/shard_map/ppermute | solution.py:388
  3.3 9.1 %collective-permute-start = (f32[32,256]{1,0:T(8,128)S(1)}, f32[32,256]{1,0:T(8,128)S(1)}, u32[]{:S(2)}, u32[]{:S(2)}) collective-permute-start(f32[32,256]{1,0:T(8,128)S(1)} %get-tuple-element.10), channel_id=1, source_target_pairs={{0,1},{1,2},{2,3},{3,4},{4,5},{5,6},{6,7},{8,9},{9,10},{10,11},{11... | collective-permute-start | bytes 98312 | tf_op jit(solution)/shard_map/ppermute | solution.py:387
  10.6 1.6 %copy-start = (f32[256,2048]{1,0:T(8,128)S(1)}, f32[256,2048]{1,0:T(8,128)}, u32[]{:S(2)}) copy-start(f32[256,2048]{1,0:T(8,128)} %coadd) | copy-start | bytes 6291460
  49.5 33.5 %copy-start.3 = (f32[256,2048]{1,0:T(8,128)S(1)}, f32[256,2048]{1,0:T(8,128)}, u32[]{:S(2)}) copy-start(f32[256,2048]{1,0:T(8,128)} %science.1) | copy-start | bytes 6291460
  49.5 33.4 %copy-start.4 = (bf16[768,512]{1,0:T(8,128)(2,1)S(1)}, bf16[768,512]{1,0:T(8,128)(2,1)}, u32[]{:S(2)}) copy-start(bf16[768,512]{1,0:T(8,128)(2,1)} %constant.8.clone.col_mat) | copy-start | bytes 2359300
  49.5 33.4 %copy-start.5 = (bf16[640,480]{1,0:T(8,128)(2,1)S(1)}, bf16[640,480]{1,0:T(8,128)(2,1)}, u32[]{:S(2)}) copy-start(bf16[640,480]{1,0:T(8,128)(2,1)} %constant.9.clone.row_mat) | copy-start | bytes 1843204
  83.0 27.0 %copy-start.1 = (bf16[256,432]{1,0:T(8,128)(2,1)S(1)}, bf16[256,432]{1,0:T(8,128)(2,1)}, u32[]{:S(2)}) copy-start(bf16[256,432]{1,0:T(8,128)(2,1)} %constant.11.clone.frow_mat) | copy-start | bytes 663556
  83.0 27.0 %copy-start.2 = (bf16[768,128]{1,0:T(8,128)(2,1)S(1)}, bf16[768,128]{1,0:T(8,128)(2,1)}, u32[]{:S(2)}) copy-start(bf16[768,128]{1,0:T(8,128)(2,1)} %constant.10.clone.fcol_mat) | copy-start | bytes 589828

commit v4 on v3

--- a/solution.py
+++ b/solution.py
@@ -98,11 +98,18 @@
     return high, (x - high.astype(f32)).astype(bf16)
 
 
-def edge_kernel(coadd_first, coadd_last, sci_first, sci_last, to_left, to_right):
-    to_left[:EDGE] = jnp.transpose(coadd_first[...])[:EDGE]
-    to_left[EDGE:] = jnp.transpose(sci_first[...])[:EDGE]
-    to_right[:EDGE] = jnp.transpose(coadd_last[...])[LANES - EDGE :]
-    to_right[EDGE:] = jnp.transpose(sci_last[...])[LANES - EDGE :]
+def edge_kernel(coadd, science, to_left, to_right, tiles, sems):
+    first, last = slice(0, LANES), slice(COLS - LANES, COLS)
+    copies = []
+    for k, (source, part) in enumerate(((coadd, first), (science, first), (coadd, last), (science, last))):
+        copies.append(pltpu.make_async_copy(source.at[:, part], tiles.at[k], sems.at[k]))
+        copies[-1].start()
+    for copy in copies:
+        copy.wait()
+    to_left[:EDGE] = jnp.transpose(tiles[0])[:EDGE]
+    to_left[EDGE:] = jnp.transpose(tiles[1])[:EDGE]
+    to_right[:EDGE] = jnp.transpose(tiles[2])[LANES - EDGE :]
+    to_right[EDGE:] = jnp.transpose(tiles[3])[LANES - EDGE :]
 
 
 def pack_kernel(tile_id, shift, coadd, out):
@@ -139,7 +146,7 @@
     keep_edges(0, BLOCKS)
     keep_edges(1, BLOCKS + 1)
 
-    def one(v, carry):
+    for v in range(BLOCKS):
         base = pl.multiple_of(meta[v, 0] * ROWS, ROWS)
         skip = meta[v, 1] - KER_HALF
         out[v, :WIN] = strip[pl.ds(base + skip, WIN), :]
@@ -147,9 +154,6 @@
         wide = pltpu.roll(wide, 5 * LANES - skip, 1)
         pieces = [wide[i : i + 1, q * LANES : (q + 1) * LANES] for i in range(2) for q in range(3)]
         out[v, WIN:] = jnp.concatenate(pieces + [wide[2:4, :LANES]], 0)
-        return carry
-
-    lax.fori_loop(0, BLOCKS, one, 0)
 
 
 def match_kernel(win, science, from_left, from_right, col_mat, row_mat, matched, sci, sums, xh, xl, acc, side):
@@ -187,11 +191,20 @@
         wide = science[:, pl.ds(at, 2 * LANES)]
         sci[t] = jnp.concatenate([wide[:, HALF:LANES], wide[:, LANES : LANES + HALF]], 1)
 
-    def rows_of(ts):
+    def rows_of(ts, steps=()):
+        steps = list(steps)
+
+        def advance():
+            if steps:
+                steps.pop(0)()
+
         for t in ts:
             if not isinstance(t, int) or 0 < t < TILES - 1:
                 frame(t)
-        ys = [layers(t) for t in ts]
+        ys = []
+        for t in ts:
+            ys.append(layers(t))
+            advance()
         for f, bases in enumerate(((0,), (1, 3), (2,), (4,))):
             lo = (0, 1, 3, 4)[f] * LANES
             lhs = row_mat[lo : lo + len(bases) * LANES, :]
@@ -204,43 +217,48 @@
                 for i, b in enumerate(bases):
                     for s, t in enumerate(ts):
                         matched[b, t, r * LANES : (r + 1) * LANES] = m[i * LANES : (i + 1) * LANES, s * LANES : (s + 1) * LANES]
-
-    def gram(tiles):
+                advance()
+        while steps:
+            advance()
+
+    def gram(tiles, count=10):
+        work = [(tile, i) for tile in tiles for i in range(ROWS // 8)]
+        size = -(-len(work) // count)
+        return [functools.partial(gram_of, work[k : k + size]) for k in range(0, len(work), size)]
+
+    def gram_of(work):
         parts = [acc[k] for k in range(26)]
-        for tile in tiles:
-            for i in range(ROWS // 8):
-                rows = slice(i * 8, i * 8 + 8)
-                if isinstance(tile, tuple):
-                    m = [jnp.where(lane >= HALF, matched[b, tile[0], rows], matched[b, tile[1], rows]) for b in range(BASIS)]
-                    d = jnp.where(lane >= HALF, sci[tile[0], rows], sci[tile[1], rows])
-                else:
-                    m = [matched[b, tile, rows] for b in range(BASIS)]
-                    d = sci[tile, rows]
-                k = 0
-                for b in range(BASIS):
-                    for c in range(b, BASIS):
-                        parts[k] = parts[k] + m[b] * m[c]
-                        k += 1
-                for b in range(BASIS):
-                    parts[15 + b] = parts[15 + b] + m[b]
-                    parts[20 + b] = parts[20 + b] + m[b] * d
-                parts[25] = parts[25] + d
+        for tile, i in work:
+            rows = slice(i * 8, i * 8 + 8)
+            if isinstance(tile, tuple):
+                m = [jnp.where(lane >= HALF, matched[b, tile[0], rows], matched[b, tile[1], rows]) for b in range(BASIS)]
+                d = jnp.where(lane >= HALF, sci[tile[0], rows], sci[tile[1], rows])
+            else:
+                m = [matched[b, tile, rows] for b in range(BASIS)]
+                d = sci[tile, rows]
+            k = 0
+            for b in range(BASIS):
+                for c in range(b, BASIS):
+                    parts[k] = parts[k] + m[b] * m[c]
+                    k += 1
+            for b in range(BASIS):
+                parts[15 + b] = parts[15 + b] + m[b]
+                parts[20 + b] = parts[20 + b] + m[b] * d
+            parts[25] = parts[25] + d
         for k in range(26):
             acc[k] = parts[k]
 
     rows_of((1, 2))
 
     def pair(p, carry):
-        gram((2 * p - 1, 2 * p))
-        rows_of((2 * p + 1, 2 * p + 2))
+        rows_of((2 * p + 1, 2 * p + 2), gram((2 * p - 1, 2 * p)))
         return carry
 
     lax.fori_loop(1, PAIRS, pair, 0)
-    gram((TILES - 4, TILES - 3))
-    rows_of((0, TILES - 1))
-    gram(((0, TILES - 1),))
-    rows_of((TILES - 2,))
-    gram((TILES - 2,))
+    rows_of((0, TILES - 1), gram((TILES - 4, TILES - 3)))
+    rows_of((TILES - 2,), gram(((0, TILES - 1),)))
+    for step in gram((TILES - 2,), 1):
+        step()
     rows = [jnp.sum(acc[k], axis=0, keepdims=True) for k in range(26)]
     rows = jnp.concatenate(rows + [jnp.zeros((NSUMS - 26, LANES), f32)], 0)
     total = jnp.broadcast_to(jnp.sum(rows, axis=1, keepdims=True), (NSUMS, LANES))
@@ -321,41 +339,55 @@
                 eh[t, r * LANES : (r + 1) * LANES] = e_hi[:, s * LANES : (s + 1) * LANES]
                 el[t, r * LANES : (r + 1) * LANES] = e_lo[:, s * LANES : (s + 1) * LANES]
 
+    def emit(j):
+        at = j * LANES if isinstance(j, int) else pl.multiple_of(j * LANES, LANES)
+        dout[:, pl.ds(at, LANES)] = jnp.concatenate([keep[j][:, HALF:], keep[j + 1][:, :HALF]], 1)
+
+    def send(source, target, first, end, sem):
+        part = slice(first * LANES, end * LANES)
+        copy = pltpu.make_async_copy(source.at[:, part], target.at[:, part], sems.at[sem])
+        copy.start()
+        return copy
+
     def pair(p, power):
         ts = (2 * p + 1, 2 * p + 2)
         ds = [residual(t) for t in ts]
         along_rows(ts, ds)
+        emit(2 * p)
+        emit(2 * p + 1)
         return power + squares(ds[0]) + squares(ds[1])
 
-    power = lax.fori_loop(0, PAIRS, pair, jnp.zeros((8, LANES), f32))
-    last = residual(TILES - 2)
-    along_rows((TILES - 2,), [last])
     low, high = residual(0), residual(TILES - 1)
-    power = power + squares(last) + squares(jnp.where(lane >= HALF, low, high))
+    power = squares(jnp.where(lane >= HALF, low, high))
     low = low * jnp.where(lane >= HALF, 1.0, low_ok)
     high = high * jnp.where(lane < HALF, 1.0, high_ok)
     along_rows((0, TILES - 1), [low, high])
+    middle = PAIRS // 2
+    power = lax.fori_loop(0, middle, pair, power)
+    copies = [send(dout, diff, 0, 2 * middle, 0)]
+    power = lax.fori_loop(middle, PAIRS, pair, power)
+    last = residual(TILES - 2)
+    along_rows((TILES - 2,), [last])
+    power = power + squares(last)
+    emit(BLOCKS - 2)
+    emit(BLOCKS - 1)
+    copies.append(send(dout, diff, 2 * middle, BLOCKS, 1))
     noise = jnp.sum(jnp.sum(power, axis=0, keepdims=True), axis=1, keepdims=True) / float(ROWS * COLS)
     scale = 1.0 / jnp.sqrt(jnp.broadcast_to(noise, (1, LANES)) + epsilon)
 
-    copies = []
+    each = BLOCKS // PARTS
     for q in range(PARTS):
-        part = slice(q * COLS // PARTS, (q + 1) * COLS // PARTS)
-        for j in range(q * BLOCKS // PARTS, (q + 1) * BLOCKS // PARTS):
+        for j in range(q * each, (q + 1) * each):
             e_hi = jnp.concatenate([eh[j], eh[j + 1]], 1)
             e_lo = jnp.concatenate([el[j], el[j + 1]], 1)
             s = jnp.dot(jnp.concatenate([e_hi, e_lo, e_hi], 1), fcol_mat[...], preferred_element_type=f32)
             sout[:, j * LANES : (j + 1) * LANES] = s * scale
-            dout[:, j * LANES : (j + 1) * LANES] = jnp.concatenate([keep[j][:, HALF:], keep[j + 1][:, :HALF]], 1)
-        copies.append(pltpu.make_async_copy(sout.at[:, part], sig.at[:, part], sems.at[2 * q]))
-        copies.append(pltpu.make_async_copy(dout.at[:, part], diff.at[:, part], sems.at[2 * q + 1]))
-        copies[-1].start()
-        copies[-2].start()
+        copies.append(send(sout, sig, q * each, (q + 1) * each, 2 + q))
     for copy in copies:
         copy.wait()
 
 
-def call(kernel, ins, outs, scratch=(), mib=8, flops=0, nbytes=0, out_specs=None, **more):
+def call(kernel, ins, outs, scratch=(), mib=12, flops=0, nbytes=0, out_specs=None, **more):
     return pl.pallas_call(
         kernel,
         out_shape=outs,
@@ -381,9 +413,13 @@
     groups = lax.axis_size(GRP)
     up, down = line(groups)
     mats = [jnp.asarray(m) for m in (COL_MAT, ROW_MAT, FCOL_MAT, FROW_MAT)]
-    to_left, to_right = call(edge_kernel, [VMEM] * 4, (shape(2 * EDGE, ROWS),) * 2)(
-        coadd[:, :LANES], coadd[:, COLS - LANES :], science[:, :LANES], science[:, COLS - LANES :]
-    )
+    to_left, to_right = call(
+        edge_kernel,
+        [pl.BlockSpec(memory_space=pl.ANY)] * 2,
+        (shape(2 * EDGE, ROWS),) * 2,
+        [pltpu.VMEM((4, ROWS, LANES), f32), pltpu.SemaphoreType.DMA((4,))],
+        mib=58,
+    )(coadd, science)
     from_left = lax.ppermute(to_right, GRP, up)
     from_right = lax.ppermute(to_left, GRP, down)
     coadd, _, _ = lax.optimization_barrier((coadd, to_left, to_right))
@@ -410,7 +446,7 @@
         (shape(BASIS, TILES, ROWS, LANES), shape(TILES, ROWS, LANES), shape(groups, 8, LANES)),
         [tile16, tile16, pltpu.VMEM((26, 8, LANES), f32), pltpu.VMEM((LANES, 3 * LANES), f32)],
         flops=8 << 30,
-        mib=12,
+        mib=24,
     )(win, science, from_left, from_right, *mats[:2])
     sums = lax.all_to_all(sums, GRP, 0, 0, tiled=True)
     block16 = pltpu.VMEM((TILES, ROWS, LANES), bf16)
@@ -421,9 +457,9 @@
         [VMEM] * 5,
         (shape(ROWS, COLS), shape(ROWS, COLS), shape(1, BASIS + 1)),
         [block16] * 2
-        + [pltpu.VMEM((TILES, ROWS, LANES), f32), image, image, pltpu.SemaphoreType.DMA((2 * PARTS,))],
+        + [pltpu.VMEM((TILES, ROWS, LANES), f32), image, image, pltpu.SemaphoreType.DMA((2 + PARTS,))],
         flops=3 << 30,
-        mib=16,
+        mib=30,
         out_specs=(anywhere, anywhere, VMEM),
     )(sums, matched, framed, *mats[2:])
 

time: 116 us -> 115 us (level)
  local copies, waits for them, and re-layouts: 2.76 us -> 0.04 us
    pallas_call x1, Pallas kernels: 0.19 us -> 2.1 us  [shards(): call(edge_kernel, [pl.BlockSpec(memory_space=pl.ANY)] * 2, (shape(2 * EDG...]
    unnamed x12, local copies, waits for them, and re-layouts: 1.62 us -> 0.04 us
    pallas_call x1, Pallas kernels: 2.27 us -> 1.1 us  [shards(): call(pick_kernel, [SMEM, VMEM], shape(BLOCKS, WIN + 8, LANES), [pltpu.VME...]
  transfers between devices with their start and end apart: 2 -> 2, of which waited for: 0 -> 1; matrix products, arithmetic and copies ran while one was open for 0% -> 0% of each run, Pallas kernels for 0% -> 0%
where the time goes in v4:
time: 115 us
  blocking collectives  83.8 us (73%)
  Pallas kernels  21.2 us (18%)
  starting transfers between devices  7.34 us (6%)
  between operations  2.04 us (2%)
    all_to_all x1, blocking collectives, shards(): held = lax.all_to_all(sent, 'visit', 0, 0, tiled=True)  34.8 us
    all_to_all x1, blocking collectives, shards(): win = lax.all_to_all(picked, 'visit', 0, 0, tiled=True)  33.4 us
    all_to_all x1, blocking collectives, shards(): sums = lax.all_to_all(sums, GRP, 0, 0, tiled=True)  15.6 us
    pallas_call x1, Pallas kernels, shards(): call(match_kernel, [VMEM] * 6, (shape(BASIS, TILES, ROWS, LANES), shape(T...  11.7 us
    pallas_call x1, Pallas kernels, shards(): call(functools.partial(finish_kernel, float(ROWS * COLS * groups), groups...  6.14 us
    ppermute x1, starting transfers between devices, shards(): from_left = lax.ppermute(to_right, GRP, up)  6.05 us
  transfers between devices with their start and end apart: 2, of which 1 were waited for; matrix products, arithmetic and copies ran while one was open for 0% of the time, Pallas kernels for 0%

profile of v4, /device:TPU:0, one launch (start us, length us, event | category | flops | bytes accessed | tf_op | source)
XLA Modules:
  0.0 114.8 jit_solution(3701337617901176)
XLA Ops:
  0.6 0.0 copy-start
  0.6 2.1 %shard_map.103 = (f32[32,256]{1,0:T(8,128)}, f32[32,256]{1,0:T(8,128)}) custom-call(f32[256,2048]{1,0:T(8,128)} %coadd.2, f32[256,2048]{1,0:T(8,128)} %science.3), custom_call_target="tpu_custom_call" | custom-call | tf_op jit(solution)/shard_map/pallas_call | solution.py:416
  2.7 1.3 %collective-permute-start.1 = (f32[32,256]{1,0:T(8,128)}, f32[32,256]{1,0:T(8,128)S(1)}, u32[]{:S(2)}, u32[]{:S(2)}) collective-permute-start(f32[32,256]{1,0:T(8,128)} %get-tuple-element.9), channel_id=1, source_target_pairs={{1,0},{2,1},{3,2},{4,3},{5,4},{6,5},{7,6},{9,8},{10,9},{11,10},{12... | collective-permute-start | bytes 98312 | tf_op jit(solution)/shard_map/ppermute | solution.py:424
  4.0 6.1 %collective-permute-start = (f32[32,256]{1,0:T(8,128)}, f32[32,256]{1,0:T(8,128)S(1)}, u32[]{:S(2)}, u32[]{:S(2)}) collective-permute-start(f32[32,256]{1,0:T(8,128)} %get-tuple-element.10), channel_id=1, source_target_pairs={{0,1},{1,2},{2,3},{3,4},{4,5},{5,6},{6,7},{8,9},{9,10},{10,11},{11... | collective-permute-start | bytes 98312 | tf_op jit(solution)/shard_map/ppermute | solution.py:423
  11.4 0.0 copy-done
  11.4 0.2 shard_map.104.packed
  11.6 0.0 collective-permute-done.1.from_right
  11.6 0.4 collective-permute-done.from_left
  12.0 34.8 %all_to_all.15.held = f32[16,264,128]{2,1,0:T(8,128)S(1)} all-to-all(f32[16,264,128]{2,1,0:T(8,128)S(1)} %shard_map.105), channel_id=1, replica_groups=mesh['visit'=16,'grp_0'=4,'grp_1'=2] {'visit'}, dimensions={0} | all-to-all | bytes 4325376 | tf_op jit(solution)/shard_map/all_to_all | solution.py:432
  46.8 1.1 shard_map.106
  47.9 0.0 copy-start.1
  47.9 0.0 copy-start.4
  47.9 0.0 copy-start.5
  47.9 33.4 %all_to_all.16.win = f32[16,288,128]{2,1,0:T(8,128)S(1)} all-to-all(f32[16,288,128]{2,1,0:T(8,128)S(1)} %shard_map.106), channel_id=1, replica_groups=mesh['visit'=16,'grp_0'=4,'grp_1'=2] {'visit'}, dimensions={0} | all-to-all | bytes 4718592 | tf_op jit(solution)/shard_map/all_to_all | solution.py:441
  81.4 0.0 copy-done.1
  81.4 0.0 copy-done.4
  81.4 0.0 copy-done.5
  81.4 0.0 copy-start.2
  81.4 0.0 copy-start.3
  81.4 11.7 %shard_map.107 = (f32[5,17,256,128]{3,2,1,0:T(8,128)S(1)}, f32[17,256,128]{2,1,0:T(8,128)S(1)}, f32[8,8,128]{2,1,0:T(8,128)S(1)}) custom-call(f32[16,288,128]{2,1,0:T(8,128)S(1)} %all_to_all.16.win, f32[256,2048]{1,0:T(8,128)S(1)} %copy-done.1, f32[32,256]{1,0:T(8,128)S(1)} %collective-permute-done.from_left, ...), custom_call_target="tpu_custom_call" | custom-call | flops 8589934592 | tf_op jit(solution)/shard_map/pallas_call | solution.py:443
  93.1 15.6 %all_to_all.17.sums = f32[8,8,128]{2,1,0:T(8,128)S(1)} all-to-all(f32[8,8,128]{2,1,0:T(8,128)S(1)} %get-tuple-element.12), channel_id=1, replica_groups=mesh['visit'=16,'grp_0'=4,'grp_1'=2] {'grp_0','grp_1'}, dimensions={0} | all-to-all | bytes 65536 | tf_op jit(solution)/shard_map/all_to_all | solution.py:451
  108.7 0.0 copy-done.2
  108.7 0.0 copy-done.3
  108.7 6.1 %shard_map.108 = (f32[256,2048]{1,0:T(8,128)}, f32[256,2048]{1,0:T(8,128)}, f32[1,6]{1,0:T(1,128)}) custom-call(f32[8,8,128]{2,1,0:T(8,128)S(1)} %all_to_all.17.sums, f32[5,17,256,128]{3,2,1,0:T(8,128)S(1)} %get-tuple-element.13.matched, f32[17,256,128]{2,1,0:T(8,128)S(1)} %get-tuple-element.14.sci, bf16[768,128]{1,0:T(8,128)(2,1)S(1)} %copy-done.3, ...), custom_call_target="tpu_custom_call" | custom-call | flops 3221225472 | tf_op jit(solution)/shard_map/pallas_call | solution.py:455
  (2 shorter events, 0.0 us)
Async XLA Ops:
  0.6 10.8 %copy-start = (f32[256,2048]{1,0:T(8,128)S(1)}, f32[256,2048]{1,0:T(8,128)}, u32[]{:S(2)}) copy-start(f32[256,2048]{1,0:T(8,128)} %coadd.2) | copy-start | bytes 6291460
  2.7 8.8 %collective-permute-start.1 = (f32[32,256]{1,0:T(8,128)}, f32[32,256]{1,0:T(8,128)S(1)}, u32[]{:S(2)}, u32[]{:S(2)}) collective-permute-start(f32[32,256]{1,0:T(8,128)} %get-tuple-element.9), channel_id=1, source_target_pairs={{1,0},{2,1},{3,2},{4,3},{5,4},{6,5},{7,6},{9,8},{10,9},{11,10},{12... | collective-permute-start | bytes 98312 | tf_op jit(solution)/shard_map/ppermute | solution.py:424
  4.0 8.0 %collective-permute-start = (f32[32,256]{1,0:T(8,128)}, f32[32,256]{1,0:T(8,128)S(1)}, u32[]{:S(2)}, u32[]{:S(2)}) collective-permute-start(f32[32,256]{1,0:T(8,128)} %get-tuple-element.10), channel_id=1, source_target_pairs={{0,1},{1,2},{2,3},{3,4},{4,5},{5,6},{6,7},{8,9},{9,10},{10,11},{11... | collective-permute-start | bytes 98312 | tf_op jit(solution)/shard_map/ppermute | solution.py:423
  47.9 33.5 %copy-start.1 = (f32[256,2048]{1,0:T(8,128)S(1)}, f32[256,2048]{1,0:T(8,128)}, u32[]{:S(2)}) copy-start(f32[256,2048]{1,0:T(8,128)} %science.3) | copy-start | bytes 6291460
  47.9 33.4 %copy-start.4 = (bf16[768,512]{1,0:T(8,128)(2,1)S(1)}, bf16[768,512]{1,0:T(8,128)(2,1)}, u32[]{:S(2)}) copy-start(bf16[768,512]{1,0:T(8,128)(2,1)} %constant.8.clone.col_mat) | copy-start | bytes 2359300
  47.9 33.4 %copy-start.5 = (bf16[640,480]{1,0:T(8,128)(2,1)S(1)}, bf16[640,480]{1,0:T(8,128)(2,1)}, u32[]{:S(2)}) copy-start(bf16[640,480]{1,0:T(8,128)(2,1)} %constant.9.clone.row_mat) | copy-start | bytes 1843204
  81.4 27.3 %copy-start.2 = (bf16[256,432]{1,0:T(8,128)(2,1)S(1)}, bf16[256,432]{1,0:T(8,128)(2,1)}, u32[]{:S(2)}) copy-start(bf16[256,432]{1,0:T(8,128)(2,1)} %constant.11.clone.frow_mat) | copy-start | bytes 663556
  81.4 27.3 %copy-start.3 = (bf16[768,128]{1,0:T(8,128)(2,1)S(1)}, bf16[768,128]{1,0:T(8,128)(2,1)}, u32[]{:S(2)}) copy-start(bf16[768,128]{1,0:T(8,128)(2,1)} %constant.10.clone.fcol_mat) | copy-start | bytes 589828

commit v5 on v4

--- a/solution.py
+++ b/solution.py
@@ -98,18 +98,11 @@
     return high, (x - high.astype(f32)).astype(bf16)
 
 
-def edge_kernel(coadd, science, to_left, to_right, tiles, sems):
-    first, last = slice(0, LANES), slice(COLS - LANES, COLS)
-    copies = []
-    for k, (source, part) in enumerate(((coadd, first), (science, first), (coadd, last), (science, last))):
-        copies.append(pltpu.make_async_copy(source.at[:, part], tiles.at[k], sems.at[k]))
-        copies[-1].start()
-    for copy in copies:
-        copy.wait()
-    to_left[:EDGE] = jnp.transpose(tiles[0])[:EDGE]
-    to_left[EDGE:] = jnp.transpose(tiles[1])[:EDGE]
-    to_right[:EDGE] = jnp.transpose(tiles[2])[LANES - EDGE :]
-    to_right[EDGE:] = jnp.transpose(tiles[3])[LANES - EDGE :]
+def edge_kernel(coadd_first, coadd_last, sci_first, sci_last, to_left, to_right):
+    to_left[:EDGE] = jnp.transpose(coadd_first[...])[:EDGE]
+    to_left[EDGE:] = jnp.transpose(sci_first[...])[:EDGE]
+    to_right[:EDGE] = jnp.transpose(coadd_last[...])[LANES - EDGE :]
+    to_right[EDGE:] = jnp.transpose(sci_last[...])[LANES - EDGE :]
 
 
 def pack_kernel(tile_id, shift, coadd, out):
@@ -120,14 +113,17 @@
         out[h, ROWS:] = meta
 
 
-def patch_kernel(packed, from_left, from_right, out):
+def patch_kernel(groups, packed, from_left, from_right, out):
+    g = lax.axis_index(GRP[0]) * lax.axis_size(GRP[1]) + lax.axis_index(GRP[1])
+    low_ok = jnp.where(g > 0, 1.0, 0.0).astype(f32)
+    high_ok = jnp.where(g < groups - 1, 1.0, 0.0).astype(f32)
     for h in range(BLOCKS):
-        source = from_left if h < BLOCKS // 2 else from_right
+        source, ok = (from_left, low_ok) if h < BLOCKS // 2 else (from_right, high_ok)
         k = 2 * h % EDGE
         for i in range(2):
             for q in range(2):
                 row = ROWS + 2 * i + q
-                out[h, row : row + 1] = source[k + i : k + i + 1, q * LANES : (q + 1) * LANES]
+                out[h, row : row + 1] = source[k + i : k + i + 1, q * LANES : (q + 1) * LANES] * ok
 
 
 def pick_kernel(meta, held, out, strip, edges):
@@ -404,29 +400,25 @@
     return jax.ShapeDtypeStruct(dims, dtype)
 
 
-def line(size):
-    up = [(i, i + 1) for i in range(size - 1)]
+def ring(size):
+    up = [(i, (i + 1) % size) for i in range(size)]
     return up, [(j, i) for i, j in up]
 
 
 def shards(coadd, science, correlation, offset):
     groups = lax.axis_size(GRP)
-    up, down = line(groups)
+    up, down = ring(groups)
     mats = [jnp.asarray(m) for m in (COL_MAT, ROW_MAT, FCOL_MAT, FROW_MAT)]
-    to_left, to_right = call(
-        edge_kernel,
-        [pl.BlockSpec(memory_space=pl.ANY)] * 2,
-        (shape(2 * EDGE, ROWS),) * 2,
-        [pltpu.VMEM((4, ROWS, LANES), f32), pltpu.SemaphoreType.DMA((4,))],
-        mib=58,
-    )(coadd, science)
+    to_left, to_right = call(edge_kernel, [VMEM] * 4, (shape(2 * EDGE, ROWS),) * 2)(
+        coadd[:, :LANES], coadd[:, COLS - LANES :], science[:, :LANES], science[:, COLS - LANES :]
+    )
     from_left = lax.ppermute(to_right, GRP, up)
     from_right = lax.ppermute(to_left, GRP, down)
     coadd, _, _ = lax.optimization_barrier((coadd, to_left, to_right))
     packed = call(pack_kernel, [SMEM, SMEM, VMEM], shape(BLOCKS, SENT, LANES), flops=1 << 20, nbytes=4 << 20)(
         correlation, offset, coadd
     )
-    sent = call(patch_kernel, [VMEM] * 3, shape(BLOCKS, SENT, LANES), input_output_aliases={0: 0})(
+    sent = call(functools.partial(patch_kernel, groups), [VMEM] * 3, shape(BLOCKS, SENT, LANES), input_output_aliases={0: 0})(
         packed, from_left, from_right
     )
     held = lax.all_to_all(sent, "visit", 0, 0, tiled=True)

time: 115 us -> 112 us (0.974)
  blocking collectives: 83.8 us -> 77.8 us
  waiting for transfers between devices: 0.41 us -> 4.46 us
  local copies, waits for them, and re-layouts: 0.04 us -> 2.76 us
  Pallas kernels: 21.2 us -> 19.3 us
  starting transfers between devices: 7.34 us -> 5.54 us
    ppermute x1, starting transfers between devices: 6.05 us -> 0.01 us  [shards(): from_left = lax.ppermute(to_right, GRP, up)]
    all_to_all x1, blocking collectives: 15.6 us -> 10.6 us  [shards(): sums = lax.all_to_all(sums, GRP, 0, 0, tiled=True)]
    ppermute x1, starting transfers between devices: 1.29 us -> 5.54 us  [shards(): from_right = lax.ppermute(to_left, GRP, down)]
    ppermute x1, waiting for transfers between devices: 0.41 us -> 4.45 us  [shards(): from_left = lax.ppermute(to_right, GRP, up)]
    pallas_call x2, Pallas kernels: 2.12 us -> 0.22 us  [the longest x1 0.19 us: shards(): call(edge_kernel, [VMEM] * 4, (shape(2 * EDGE, ROWS),) * 2)]
    unnamed x12, local copies, waits for them, and re-layouts: 0.04 us -> 1.62 us
where the time goes in v5:
time: 112 us
  blocking collectives  77.8 us (69%)
  Pallas kernels  19.3 us (17%)
  starting transfers between devices  5.54 us (5%)
  waiting for transfers between devices  4.46 us (4%)
  local copies, waits for them, and re-layouts  2.76 us (2%)
  between operations  2.03 us (2%)
    all_to_all x1, blocking collectives, shards(): held = lax.all_to_all(sent, 'visit', 0, 0, tiled=True)  33.8 us
    all_to_all x1, blocking collectives, shards(): win = lax.all_to_all(picked, 'visit', 0, 0, tiled=True)  33.4 us
    pallas_call x1, Pallas kernels, shards(): call(match_kernel, [VMEM] * 6, (shape(BASIS, TILES, ROWS, LANES), shape(T...  11.7 us
    all_to_all x1, blocking collectives, shards(): sums = lax.all_to_all(sums, GRP, 0, 0, tiled=True)  10.6 us
    pallas_call x1, Pallas kernels, shards(): call(functools.partial(finish_kernel, float(ROWS * COLS * groups), groups...  6.14 us
    ppermute x1, starting transfers between devices, shards(): from_right = lax.ppermute(to_left, GRP, down)  5.54 us
    ppermute x1, waiting for transfers between devices, shards(): from_left = lax.ppermute(to_right, GRP, up)  4.45 us
  transfers between devices with their start and end apart: 2, of which 1 were waited for; matrix products, arithmetic and copies ran while one was open for 0% of the time, Pallas kernels for 0%

profile of v5, /device:TPU:0, one launch (start us, length us, event | category | flops | bytes accessed | tf_op | source)
XLA Modules:
  0.0 111.9 jit_solution(9226079072471803616)
XLA Ops:
  0.6 1.1 %fusion = (f32[256,128]{1,0:T(8,128)S(1)}, f32[256,128]{1,0:T(8,128)S(1)}, f32[256,128]{1,0:T(8,128)S(1)}, f32[256,128]{1,0:T(8,128)S(1)}) fusion(f32[256,2048]{1,0:T(8,128)} %science.1, f32[256,2048]{1,0:T(8,128)} %coadd), kind=kLoop, calls=%fused_computation.1 | loop fusion | bytes 1048576 | tf_op jit(solution)/shard_map/slice | solution.py:413
  1.8 0.2 shard_map.103
  2.0 5.5 %collective-permute-start.1 = (f32[32,256]{1,0:T(8,128)S(1)}, f32[32,256]{1,0:T(8,128)S(1)}, u32[]{:S(2)}, u32[]{:S(2)}) collective-permute-start(f32[32,256]{1,0:T(8,128)S(1)} %get-tuple-element.9), channel_id=1, source_target_pairs={{1,0},{2,1},{3,2},{4,3},{5,4},{6,5},{7,6},{0,7},{9,8},{10,9},{11,1... | collective-permute-start | bytes 98312 | tf_op jit(solution)/shard_map/ppermute | solution.py:416
  7.5 0.0 collective-permute-start
  8.8 0.0 copy-start
  8.8 1.6 %copy-done = f32[256,2048]{1,0:T(8,128)S(1)} copy-done((f32[256,2048]{1,0:T(8,128)S(1)}, f32[256,2048]{1,0:T(8,128)}, u32[]{:S(2)}) %copy-start) | copy-done | bytes 2097176
  10.4 0.2 shard_map.104.packed
  10.6 0.0 collective-permute-done.1.from_right
  10.6 4.5 %collective-permute-done.from_left = f32[32,256]{1,0:T(8,128)S(1)} collective-permute-done((f32[32,256]{1,0:T(8,128)S(1)}, f32[32,256]{1,0:T(8,128)S(1)}, u32[]{:S(2)}, u32[]{:S(2)}) %collective-permute-start) | collective-permute-done | bytes 32800 | tf_op jit(solution)/shard_map/ppermute | solution.py:415
  15.1 33.8 %all_to_all.15.held = f32[16,264,128]{2,1,0:T(8,128)S(1)} all-to-all(f32[16,264,128]{2,1,0:T(8,128)S(1)} %shard_map.105), channel_id=1, replica_groups=mesh['visit'=16,'grp_0'=4,'grp_1'=2] {'visit'}, dimensions={0} | all-to-all | bytes 4325376 | tf_op jit(solution)/shard_map/all_to_all | solution.py:424
  48.9 1.1 shard_map.106
  50.0 0.0 copy-start.3
  50.0 0.0 copy-start.4
  50.0 0.0 copy-start.5
  50.0 33.4 %all_to_all.16.win = f32[16,288,128]{2,1,0:T(8,128)S(1)} all-to-all(f32[16,288,128]{2,1,0:T(8,128)S(1)} %shard_map.106), channel_id=1, replica_groups=mesh['visit'=16,'grp_0'=4,'grp_1'=2] {'visit'}, dimensions={0} | all-to-all | bytes 4718592 | tf_op jit(solution)/shard_map/all_to_all | solution.py:433
  83.4 0.0 copy-done.3
  83.4 0.0 copy-done.4
  83.4 0.0 copy-done.5
  83.4 0.0 copy-start.1
  83.4 0.0 copy-start.2
  83.5 11.7 %shard_map.107 = (f32[5,17,256,128]{3,2,1,0:T(8,128)S(1)}, f32[17,256,128]{2,1,0:T(8,128)S(1)}, f32[8,8,128]{2,1,0:T(8,128)S(1)}) custom-call(f32[16,288,128]{2,1,0:T(8,128)S(1)} %all_to_all.16.win, f32[256,2048]{1,0:T(8,128)S(1)} %copy-done.3, f32[32,256]{1,0:T(8,128)S(1)} %collective-permute-done.from_left, ...), custom_call_target="tpu_custom_call" | custom-call | flops 8589934592 | tf_op jit(solution)/shard_map/pallas_call | solution.py:435
  95.2 10.6 %all_to_all.17.sums = f32[8,8,128]{2,1,0:T(8,128)S(1)} all-to-all(f32[8,8,128]{2,1,0:T(8,128)S(1)} %get-tuple-element.12), channel_id=1, replica_groups=mesh['visit'=16,'grp_0'=4,'grp_1'=2] {'grp_0','grp_1'}, dimensions={0} | all-to-all | bytes 65536 | tf_op jit(solution)/shard_map/all_to_all | solution.py:443
  105.8 0.0 copy-done.1
  105.8 0.0 copy-done.2
  105.8 6.1 %shard_map.108 = (f32[256,2048]{1,0:T(8,128)}, f32[256,2048]{1,0:T(8,128)}, f32[1,6]{1,0:T(1,128)}) custom-call(f32[8,8,128]{2,1,0:T(8,128)S(1)} %all_to_all.17.sums, f32[5,17,256,128]{3,2,1,0:T(8,128)S(1)} %get-tuple-element.13.matched, f32[17,256,128]{2,1,0:T(8,128)S(1)} %get-tuple-element.14.sci, bf16[768,128]{1,0:T(8,128)(2,1)S(1)} %copy-done.2, ...), custom_call_target="tpu_custom_call" | custom-call | flops 3221225472 | tf_op jit(solution)/shard_map/pallas_call | solution.py:447
  (2 shorter events, 0.0 us)
Async XLA Ops:
  2.0 8.6 %collective-permute-start.1 = (f32[32,256]{1,0:T(8,128)S(1)}, f32[32,256]{1,0:T(8,128)S(1)}, u32[]{:S(2)}, u32[]{:S(2)}) collective-permute-start(f32[32,256]{1,0:T(8,128)S(1)} %get-tuple-element.9), channel_id=1, source_target_pairs={{1,0},{2,1},{3,2},{4,3},{5,4},{6,5},{7,6},{0,7},{9,8},{10,9},{11,1... | collective-permute-start | bytes 98312 | tf_op jit(solution)/shard_map/ppermute | solution.py:416
  7.5 7.5 %collective-permute-start = (f32[32,256]{1,0:T(8,128)S(1)}, f32[32,256]{1,0:T(8,128)S(1)}, u32[]{:S(2)}, u32[]{:S(2)}) collective-permute-start(f32[32,256]{1,0:T(8,128)S(1)} %get-tuple-element.10), channel_id=1, source_target_pairs={{0,1},{1,2},{2,3},{3,4},{4,5},{5,6},{6,7},{7,0},{8,9},{9,10},{10,1... | collective-permute-start | bytes 98312 | tf_op jit(solution)/shard_map/ppermute | solution.py:415
  8.8 1.6 %copy-start = (f32[256,2048]{1,0:T(8,128)S(1)}, f32[256,2048]{1,0:T(8,128)}, u32[]{:S(2)}) copy-start(f32[256,2048]{1,0:T(8,128)} %coadd) | copy-start | bytes 6291460
  50.0 33.5 %copy-start.3 = (f32[256,2048]{1,0:T(8,128)S(1)}, f32[256,2048]{1,0:T(8,128)}, u32[]{:S(2)}) copy-start(f32[256,2048]{1,0:T(8,128)} %science.1) | copy-start | bytes 6291460
  50.0 33.4 %copy-start.4 = (bf16[768,512]{1,0:T(8,128)(2,1)S(1)}, bf16[768,512]{1,0:T(8,128)(2,1)}, u32[]{:S(2)}) copy-start(bf16[768,512]{1,0:T(8,128)(2,1)} %constant.8.clone.col_mat) | copy-start | bytes 2359300
  50.0 33.4 %copy-start.5 = (bf16[640,480]{1,0:T(8,128)(2,1)S(1)}, bf16[640,480]{1,0:T(8,128)(2,1)}, u32[]{:S(2)}) copy-start(bf16[640,480]{1,0:T(8,128)(2,1)} %constant.9.clone.row_mat) | copy-start | bytes 1843204
  83.4 22.3 %copy-start.1 = (bf16[256,432]{1,0:T(8,128)(2,1)S(1)}, bf16[256,432]{1,0:T(8,128)(2,1)}, u32[]{:S(2)}) copy-start(bf16[256,432]{1,0:T(8,128)(2,1)} %constant.11.clone.frow_mat) | copy-start | bytes 663556
  83.4 22.3 %copy-start.2 = (bf16[768,128]{1,0:T(8,128)(2,1)S(1)}, bf16[768,128]{1,0:T(8,128)(2,1)}, u32[]{:S(2)}) copy-start(bf16[768,128]{1,0:T(8,128)(2,1)} %constant.10.clone.fcol_mat) | copy-start | bytes 589828

commit v6 on v5

--- a/solution.py
+++ b/solution.py
@@ -359,9 +359,11 @@
     high = high * jnp.where(lane < HALF, 1.0, high_ok)
     along_rows((0, TILES - 1), [low, high])
     middle = PAIRS // 2
-    power = lax.fori_loop(0, middle, pair, power)
+    for p in range(middle):
+        power = pair(p, power)
     copies = [send(dout, diff, 0, 2 * middle, 0)]
-    power = lax.fori_loop(middle, PAIRS, pair, power)
+    for p in range(middle, PAIRS):
+        power = pair(p, power)
     last = residual(TILES - 2)
     along_rows((TILES - 2,), [last])
     power = power + squares(last)

time: 112 us -> 111 us (level)
    pallas_call x1, Pallas kernels: 6.14 us -> 5.01 us  [shards(): call(functools.partial(finish_kernel, float(ROWS * COLS * groups), groups...]
where the time goes in v6:
time: 111 us
  blocking collectives  77.8 us (70%)
  Pallas kernels  18.2 us (16%)
  starting transfers between devices  5.54 us (5%)
  waiting for transfers between devices  4.46 us (4%)
  local copies, waits for them, and re-layouts  2.76 us (2%)
  between operations  2.03 us (2%)
    all_to_all x1, blocking collectives, shards(): held = lax.all_to_all(sent, 'visit', 0, 0, tiled=True)  33.8 us
    all_to_all x1, blocking collectives, shards(): win = lax.all_to_all(picked, 'visit', 0, 0, tiled=True)  33.4 us
    pallas_call x1, Pallas kernels, shards(): call(match_kernel, [VMEM] * 6, (shape(BASIS, TILES, ROWS, LANES), shape(T...  11.7 us
    all_to_all x1, blocking collectives, shards(): sums = lax.all_to_all(sums, GRP, 0, 0, tiled=True)  10.6 us
    ppermute x1, starting transfers between devices, shards(): from_right = lax.ppermute(to_left, GRP, down)  5.54 us
    pallas_call x1, Pallas kernels, shards(): call(functools.partial(finish_kernel, float(ROWS * COLS * groups), groups...  5.01 us
    ppermute x1, waiting for transfers between devices, shards(): from_left = lax.ppermute(to_right, GRP, up)  4.45 us
  transfers between devices with their start and end apart: 2, of which 1 were waited for; matrix products, arithmetic and copies ran while one was open for 0% of the time, Pallas kernels for 0%

profile of v6, /device:TPU:0, one launch (start us, length us, event | category | flops | bytes accessed | tf_op | source)
XLA Modules:
  0.0 110.8 jit_solution(14686810766339758149)
XLA Ops:
  0.6 1.1 %fusion = (f32[256,128]{1,0:T(8,128)S(1)}, f32[256,128]{1,0:T(8,128)S(1)}, f32[256,128]{1,0:T(8,128)S(1)}, f32[256,128]{1,0:T(8,128)S(1)}) fusion(f32[256,2048]{1,0:T(8,128)} %science.1, f32[256,2048]{1,0:T(8,128)} %coadd), kind=kLoop, calls=%fused_computation.1 | loop fusion | bytes 1048576 | tf_op jit(solution)/shard_map/slice | solution.py:415
  1.8 0.2 shard_map.103
  2.0 5.5 %collective-permute-start.1 = (f32[32,256]{1,0:T(8,128)S(1)}, f32[32,256]{1,0:T(8,128)S(1)}, u32[]{:S(2)}, u32[]{:S(2)}) collective-permute-start(f32[32,256]{1,0:T(8,128)S(1)} %get-tuple-element.9), channel_id=1, source_target_pairs={{1,0},{2,1},{3,2},{4,3},{5,4},{6,5},{7,6},{0,7},{9,8},{10,9},{11,1... | collective-permute-start | bytes 98312 | tf_op jit(solution)/shard_map/ppermute | solution.py:418
  7.5 0.0 collective-permute-start
  8.8 0.0 copy-start
  8.8 1.6 %copy-done = f32[256,2048]{1,0:T(8,128)S(1)} copy-done((f32[256,2048]{1,0:T(8,128)S(1)}, f32[256,2048]{1,0:T(8,128)}, u32[]{:S(2)}) %copy-start) | copy-done | bytes 2097176
  10.4 0.2 shard_map.104.packed
  10.6 0.0 collective-permute-done.1.from_right
  10.6 4.5 %collective-permute-done.from_left = f32[32,256]{1,0:T(8,128)S(1)} collective-permute-done((f32[32,256]{1,0:T(8,128)S(1)}, f32[32,256]{1,0:T(8,128)S(1)}, u32[]{:S(2)}, u32[]{:S(2)}) %collective-permute-start) | collective-permute-done | bytes 32800 | tf_op jit(solution)/shard_map/ppermute | solution.py:417
  15.1 33.8 %all_to_all.15.held = f32[16,264,128]{2,1,0:T(8,128)S(1)} all-to-all(f32[16,264,128]{2,1,0:T(8,128)S(1)} %shard_map.105), channel_id=1, replica_groups=mesh['visit'=16,'grp_0'=4,'grp_1'=2] {'visit'}, dimensions={0} | all-to-all | bytes 4325376 | tf_op jit(solution)/shard_map/all_to_all | solution.py:426
  48.9 1.1 shard_map.106
  50.0 0.0 copy-start.3
  50.0 0.0 copy-start.4
  50.0 0.0 copy-start.5
  50.0 33.4 %all_to_all.16.win = f32[16,288,128]{2,1,0:T(8,128)S(1)} all-to-all(f32[16,288,128]{2,1,0:T(8,128)S(1)} %shard_map.106), channel_id=1, replica_groups=mesh['visit'=16,'grp_0'=4,'grp_1'=2] {'visit'}, dimensions={0} | all-to-all | bytes 4718592 | tf_op jit(solution)/shard_map/all_to_all | solution.py:435
  83.4 0.0 copy-done.3
  83.4 0.0 copy-done.4
  83.4 0.0 copy-done.5
  83.4 0.0 copy-start.1
  83.4 0.0 copy-start.2
  83.5 11.7 %shard_map.107 = (f32[5,17,256,128]{3,2,1,0:T(8,128)S(1)}, f32[17,256,128]{2,1,0:T(8,128)S(1)}, f32[8,8,128]{2,1,0:T(8,128)S(1)}) custom-call(f32[16,288,128]{2,1,0:T(8,128)S(1)} %all_to_all.16.win, f32[256,2048]{1,0:T(8,128)S(1)} %copy-done.3, f32[32,256]{1,0:T(8,128)S(1)} %collective-permute-done.from_left, ...), custom_call_target="tpu_custom_call" | custom-call | flops 8589934592 | tf_op jit(solution)/shard_map/pallas_call | solution.py:437
  95.2 10.6 %all_to_all.17.sums = f32[8,8,128]{2,1,0:T(8,128)S(1)} all-to-all(f32[8,8,128]{2,1,0:T(8,128)S(1)} %get-tuple-element.12), channel_id=1, replica_groups=mesh['visit'=16,'grp_0'=4,'grp_1'=2] {'grp_0','grp_1'}, dimensions={0} | all-to-all | bytes 65536 | tf_op jit(solution)/shard_map/all_to_all | solution.py:445
  105.8 0.0 copy-done.1
  105.8 0.0 copy-done.2
  105.8 5.0 %shard_map.108 = (f32[256,2048]{1,0:T(8,128)}, f32[256,2048]{1,0:T(8,128)}, f32[1,6]{1,0:T(1,128)}) custom-call(f32[8,8,128]{2,1,0:T(8,128)S(1)} %all_to_all.17.sums, f32[5,17,256,128]{3,2,1,0:T(8,128)S(1)} %get-tuple-element.13.matched, f32[17,256,128]{2,1,0:T(8,128)S(1)} %get-tuple-element.14.sci, bf16[768,128]{1,0:T(8,128)(2,1)S(1)} %copy-done.2, ...), custom_call_target="tpu_custom_call" | custom-call | flops 3221225472 | tf_op jit(solution)/shard_map/pallas_call | solution.py:449
  (2 shorter events, 0.0 us)
Async XLA Ops:
  2.0 8.6 %collective-permute-start.1 = (f32[32,256]{1,0:T(8,128)S(1)}, f32[32,256]{1,0:T(8,128)S(1)}, u32[]{:S(2)}, u32[]{:S(2)}) collective-permute-start(f32[32,256]{1,0:T(8,128)S(1)} %get-tuple-element.9), channel_id=1, source_target_pairs={{1,0},{2,1},{3,2},{4,3},{5,4},{6,5},{7,6},{0,7},{9,8},{10,9},{11,1... | collective-permute-start | bytes 98312 | tf_op jit(solution)/shard_map/ppermute | solution.py:418
  7.5 7.5 %collective-permute-start = (f32[32,256]{1,0:T(8,128)S(1)}, f32[32,256]{1,0:T(8,128)S(1)}, u32[]{:S(2)}, u32[]{:S(2)}) collective-permute-start(f32[32,256]{1,0:T(8,128)S(1)} %get-tuple-element.10), channel_id=1, source_target_pairs={{0,1},{1,2},{2,3},{3,4},{4,5},{5,6},{6,7},{7,0},{8,9},{9,10},{10,1... | collective-permute-start | bytes 98312 | tf_op jit(solution)/shard_map/ppermute | solution.py:417
  8.8 1.6 %copy-start = (f32[256,2048]{1,0:T(8,128)S(1)}, f32[256,2048]{1,0:T(8,128)}, u32[]{:S(2)}) copy-start(f32[256,2048]{1,0:T(8,128)} %coadd) | copy-start | bytes 6291460
  50.0 33.5 %copy-start.3 = (f32[256,2048]{1,0:T(8,128)S(1)}, f32[256,2048]{1,0:T(8,128)}, u32[]{:S(2)}) copy-start(f32[256,2048]{1,0:T(8,128)} %science.1) | copy-start | bytes 6291460
  50.0 33.4 %copy-start.4 = (bf16[768,512]{1,0:T(8,128)(2,1)S(1)}, bf16[768,512]{1,0:T(8,128)(2,1)}, u32[]{:S(2)}) copy-start(bf16[768,512]{1,0:T(8,128)(2,1)} %constant.8.clone.col_mat) | copy-start | bytes 2359300
  50.0 33.4 %copy-start.5 = (bf16[640,480]{1,0:T(8,128)(2,1)S(1)}, bf16[640,480]{1,0:T(8,128)(2,1)}, u32[]{:S(2)}) copy-start(bf16[640,480]{1,0:T(8,128)(2,1)} %constant.9.clone.row_mat) | copy-start | bytes 1843204
  83.4 22.3 %copy-start.1 = (bf16[256,432]{1,0:T(8,128)(2,1)S(1)}, bf16[256,432]{1,0:T(8,128)(2,1)}, u32[]{:S(2)}) copy-start(bf16[256,432]{1,0:T(8,128)(2,1)} %constant.11.clone.frow_mat) | copy-start | bytes 663556
  83.4 22.3 %copy-start.2 = (bf16[768,128]{1,0:T(8,128)(2,1)S(1)}, bf16[768,128]{1,0:T(8,128)(2,1)}, u32[]{:S(2)}) copy-start(bf16[768,128]{1,0:T(8,128)(2,1)} %constant.10.clone.fcol_mat) | copy-start | bytes 589828
